TPU v7x, 32 devices: a whole 2x2x4 slice. The times are simulated.
32 devices in a mesh: dp: 8 (over z, x), tensor: 4 (over y, core).
Axes of the slice: x: 2, y: 2, z: 4, core: 2. Of those that a mesh axis runs over, the one named last changes fastest.
Arguments:
- image_tokens: bfloat16 [12608, 768], P('dp'), may hold values from -6 to 6
- image_count: int32 [8], P('dp'), may hold values from 1 to 8, as said below
- expert_routes: int32 [12608, 2], P('dp'), may hold values from 0 to 7, all different within a row; in each aligned block of 1576 rows (0 to 1575, 1576 to 3151, ...) at most 396 rows name the same one
- out_cotangent: bfloat16 [12608, 768], P('dp'), may hold values from -6 to 6
- norm_gains: float32 [2, 2, 768], replicated, may hold values from 0.5 to 1.5
- attn_qkv: bfloat16 [2, 3, 768, 768], P(None, None, None, 'tensor'), may hold values from -0.21875 to 0.21875
- attn_proj: bfloat16 [2, 768, 768], P(None, 'tensor'), may hold values from -2 to 2
- dense_up: bfloat16 [768, 3072], P(None, 'tensor'), may hold values from -0.21875 to 0.21875
- dense_down: bfloat16 [3072, 768], P('tensor'), may hold values from -0.109375 to 0.109375
- router_weight: float32 [768, 8], replicated, may hold values from -0.15625 to 0.15625
- expert_up: bfloat16 [8, 768, 3072], P('dp', None, 'tensor'), may hold values from -0.21875 to 0.21875
- expert_down: bfloat16 [8, 3072, 768], P('dp', 'tensor'), may hold values from -1.25 to 1.25
Outputs:
- block_output: bfloat16 [12608, 768], P('dp')
- input_grad: float32 [12608, 768], P('dp')
- gains_grad: float32 [2, 2, 768], replicated
- qkv_grad: float32 [2, 3, 768, 768], P(None, None, None, 'tensor')
- proj_grad: float32 [2, 768, 768], P(None, 'tensor')
- up_grad: float32 [768, 3072], P(None, 'tensor')
- down_grad: float32 [3072, 768], P('tensor')
- router_grad: float32 [768, 8], replicated
- expert_up_grad: float32 [8, 768, 3072], P('dp', None, 'tensor')
- expert_down_grad: float32 [8, 3072, 768], P('dp', 'tensor')
Inputs may be any that keep to these rules, and one draw needn't show every extreme that they name: `expert_routes`: each row names two different experts. Among the rows of one index of dp no expert is named more than 396 times, a bound that some block reaches. Index d of dp holds image_count[d] live images in its first slots, the others are padding whose tokens go to no expert; some index has all 8 slots live.
All inputs are finite; a program needn't handle non-finite values.
Results may differ from a plain program's by a relative error of at most 0.028.
The roundings to bfloat16 on the way count: a program that leaves them out, or rounds other values in their place, can miss the bound.
Values may be sent and summed in bfloat16 or wider, within the bound.
No kernel may reach another device: no remote copies, remote signals or barrier semaphores. Data moves between devices by JAX's collectives and lax.ppermute only.
A program may use at most 256 MiB of HBM per device.

v0:
```python
import jax
import jax.numpy as jnp
from jax import lax
from jax.sharding import PartitionSpec as P

HD = 64
SEQ = 197


epsilon = 1e-06
highest = lax.Precision.HIGHEST


def matmul(left_side, right_side):
    return jnp.dot(left_side, right_side, preferred_element_type=jnp.float32)


def matmul_tn(left_side, right_side):
    return lax.dot_general(
        left_side, right_side, (((0,), (0,)), ((), ())), preferred_element_type=jnp.float32
    )


def matmul_nt(left_side, right_side):
    return lax.dot_general(
        left_side, right_side, (((1,), (1,)), ((), ())), preferred_element_type=jnp.float32
    )


def tensor_total(term_rows, tokens):
    return lax.psum(term_rows(0, tokens), "tensor")


def norm_forward(values, norm_gain):
    centered = values - jnp.mean(values, axis=-1, keepdims=True)
    inverse = lax.rsqrt(jnp.mean(centered * centered, axis=-1, keepdims=True) + epsilon)
    unit_rows = centered * inverse
    return (unit_rows * norm_gain, unit_rows, inverse)


def norm_backward(grad_out, norm_gain, unit_rows, inverse):
    grad_unit = grad_out * norm_gain
    grad_in = inverse * (
        grad_unit
        - jnp.mean(grad_unit, axis=-1, keepdims=True)
        - unit_rows * jnp.mean(grad_unit * unit_rows, axis=-1, keepdims=True)
    )
    return (grad_in, jnp.sum(grad_out * unit_rows, axis=0))


def attention_forward(stream, norm_gain, qkv_w, proj_w):
    normed, unit_rows, inverse = norm_forward(stream, norm_gain)
    normed_b = normed.astype(jnp.bfloat16)
    tokens = normed_b.shape[0]
    images = tokens // SEQ
    heads_dev = qkv_w.shape[2] // HD
    projected = jnp.einsum("td,jdc->jtc", normed_b, qkv_w, preferred_element_type=jnp.float32)
    rounded = projected.astype(jnp.bfloat16).reshape(3, images, SEQ, heads_dev, HD)
    queries, key_rows, value_rows = (rounded[0], rounded[1], rounded[2])
    scores = jnp.einsum(
        "ishd,ithd->ihst", queries, key_rows, preferred_element_type=jnp.float32
    ) * HD ** (-0.5)
    row_peak = jnp.max(scores, axis=-1, keepdims=True)
    weights = jnp.exp(scores - row_peak)
    row_total = jnp.sum(weights, axis=-1, keepdims=True)
    log_total = row_peak + jnp.log(row_total)
    weights_b = (weights / row_total).astype(jnp.bfloat16)
    context = jnp.einsum(
        "ihst,ithd->ishd", weights_b, value_rows, preferred_element_type=jnp.float32
    )
    context = context.astype(jnp.bfloat16).reshape(tokens, -1)

    def attention_out_rows(start, count):
        return matmul(context, proj_w)

    branch = tensor_total(attention_out_rows, tokens)
    return (
        stream + branch,
        (unit_rows, inverse, normed_b, queries, key_rows, value_rows, log_total, context),
    )


def attention_backward(grad_stream, norm_gain, qkv_w, proj_w, saved_state):
    unit_rows, inverse, normed_b, queries, key_rows, value_rows, log_total, context = saved_state
    tokens = normed_b.shape[0]
    grad_branch = grad_stream.astype(jnp.bfloat16)
    grad_proj = matmul_tn(context, grad_branch)
    grad_context = matmul_nt(grad_branch, proj_w).astype(jnp.bfloat16).reshape(queries.shape)
    scores = jnp.einsum(
        "ishd,ithd->ihst", queries, key_rows, preferred_element_type=jnp.float32
    ) * HD ** (-0.5)
    probs_again = jnp.exp(scores - log_total)
    grad_weights = jnp.einsum(
        "ishd,ithd->ihst", grad_context, value_rows, preferred_element_type=jnp.float32
    )
    grad_values = jnp.einsum(
        "ihst,ishd->ithd",
        probs_again.astype(jnp.bfloat16),
        grad_context,
        preferred_element_type=jnp.float32,
    )
    grad_scores = probs_again * (
        grad_weights - jnp.sum(probs_again * grad_weights, axis=-1, keepdims=True)
    )
    grad_scores = grad_scores.astype(jnp.bfloat16)
    grad_queries = jnp.einsum(
        "ihst,ithd->ishd", grad_scores, key_rows, preferred_element_type=jnp.float32
    ) * HD ** (-0.5)
    grad_keys = jnp.einsum(
        "ihst,ishd->ithd", grad_scores, queries, preferred_element_type=jnp.float32
    ) * HD ** (-0.5)
    stacked = (
        jnp.stack([grad_queries, grad_keys, grad_values])
        .astype(jnp.bfloat16)
        .reshape(3, tokens, -1)
    )
    grad_qkv = jnp.einsum("td,jtc->jdc", normed_b, stacked, preferred_element_type=jnp.float32)

    def attention_normed_rows(start, count):
        return jnp.einsum("jtc,jdc->td", stacked, qkv_w, preferred_element_type=jnp.float32)

    grad_normed = tensor_total(attention_normed_rows, tokens)
    grad_in, grad_gain = norm_backward(grad_normed, norm_gain, unit_rows, inverse)
    return (grad_stream + grad_in, grad_qkv, grad_proj, grad_gain)


def dense_forward(stream, norm_gain, up_w, down_w):
    normed, unit_rows, inverse = norm_forward(stream, norm_gain)
    normed_b = normed.astype(jnp.bfloat16)
    tokens = normed_b.shape[0]
    hidden_pre = matmul(normed_b, up_w)
    hidden_b = jax.nn.gelu(hidden_pre).astype(jnp.bfloat16)

    def dense_out_rows(start, count):
        return matmul(hidden_b, down_w)

    branch = tensor_total(dense_out_rows, tokens)
    return (stream + branch, (unit_rows, inverse, normed_b, hidden_pre, hidden_b))


def dense_backward(grad_stream, norm_gain, up_w, down_w, saved_state):
    unit_rows, inverse, normed_b, hidden_pre, hidden_b = saved_state
    tokens = normed_b.shape[0]
    grad_branch = grad_stream.astype(jnp.bfloat16)
    grad_down = matmul_tn(hidden_b, grad_branch)
    unused_out, gelu_back = jax.vjp(jax.nn.gelu, hidden_pre)
    grad_pre = gelu_back(matmul_nt(grad_branch, down_w))[0].astype(jnp.bfloat16)
    grad_up = matmul_tn(normed_b, grad_pre)

    def dense_normed_rows(start, count):
        return matmul_nt(grad_pre, up_w)

    grad_normed = tensor_total(dense_normed_rows, tokens)
    grad_in, grad_gain = norm_backward(grad_normed, norm_gain, unit_rows, inverse)
    return (grad_stream + grad_in, grad_up, grad_down, grad_gain)


def dispatch(send_rows):
    arrived = lax.all_to_all(send_rows, "dp", split_axis=0, concat_axis=0, tiled=True)
    return arrived.reshape(-1, send_rows.shape[2])


def give_back(partial_out, capacity):
    sources = partial_out.shape[0] // capacity
    summed_rows = lax.psum(partial_out.astype(jnp.bfloat16), "tensor")
    arrived = lax.all_to_all(
        summed_rows.reshape(sources, capacity, -1), "dp", split_axis=0, concat_axis=0, tiled=True
    )
    return arrived.reshape(-1, partial_out.shape[1])


def scatter_rows(row_values, slot_index, rows_total):
    buffer_rows = jnp.zeros((rows_total + 1, row_values.shape[-1]), jnp.bfloat16)
    buffer_rows = buffer_rows.at[slot_index.reshape(-1)].set(
        row_values.reshape(-1, row_values.shape[-1])
    )
    return buffer_rows[:-1]


def pick_rows(buffer_rows, slot_index):
    padded = jnp.concatenate(
        [buffer_rows, jnp.zeros((1, buffer_rows.shape[1]), jnp.bfloat16)], axis=0
    )
    return padded[slot_index]


def expert_forward(stream, norm_gain, router_w, up_w, down_w, routes, live_count):
    normed, unit_rows, inverse = norm_forward(stream, norm_gain)
    normed_b = normed.astype(jnp.bfloat16)
    tokens = normed_b.shape[0]
    experts = router_w.shape[1]
    dp_size = lax.axis_size("dp")
    capacity = (2 * tokens + dp_size - 1) // dp_size + 2
    logits = jnp.dot(normed_b.astype(jnp.float32), router_w, precision=highest)
    gate_probs = jax.nn.softmax(logits, axis=-1)
    live_rows = jnp.arange(tokens, dtype=jnp.int32) // SEQ < live_count[0]
    chosen = routes[..., None] == jnp.arange(experts, dtype=jnp.int32)
    kept_pairs = chosen & live_rows[:, None, None]
    gate_values = jnp.sum(jnp.where(kept_pairs, gate_probs[:, None, :], 0.0), axis=-1)
    pair_flags = kept_pairs.reshape(tokens * 2, experts).astype(jnp.int32)
    slot_rank = jnp.sum((jnp.cumsum(pair_flags, axis=0) - pair_flags) * pair_flags, axis=-1)
    slot_index = jnp.where(
        live_rows[:, None], routes * capacity + slot_rank.reshape(tokens, 2), experts * capacity
    )
    doubled = jnp.broadcast_to(normed_b[:, None, :], (tokens, 2, normed_b.shape[1]))
    send_rows = scatter_rows(doubled, slot_index, experts * capacity).reshape(experts, capacity, -1)
    rows_in = dispatch(send_rows)
    hidden_pre = matmul(rows_in, up_w[0])
    hidden_b = jax.nn.gelu(hidden_pre).astype(jnp.bfloat16)
    returned = give_back(matmul(hidden_b, down_w[0]), capacity)
    picked = pick_rows(returned, slot_index)
    branch = jnp.sum(gate_values[..., None] * picked.astype(jnp.float32), axis=1)
    saved_state = (
        unit_rows,
        inverse,
        normed_b,
        gate_probs,
        kept_pairs,
        gate_values,
        slot_index,
        rows_in,
        hidden_pre,
        hidden_b,
        picked,
        capacity,
    )
    return (stream + branch, saved_state)


def expert_backward(grad_full, grad_stream, norm_gain, router_w, up_w, down_w, saved_state):
    (
        unit_rows,
        inverse,
        normed_b,
        gate_probs,
        kept_pairs,
        gate_values,
        slot_index,
        rows_in,
        hidden_pre,
        hidden_b,
        picked,
        capacity,
    ) = saved_state
    experts = router_w.shape[1]
    grad_gates = jnp.sum(grad_full[:, None, :] * picked.astype(jnp.float32), axis=-1)
    grad_pairs = (gate_values[..., None] * grad_full[:, None, :]).astype(jnp.bfloat16)
    back_rows = scatter_rows(grad_pairs, slot_index, experts * capacity).reshape(
        experts, capacity, -1
    )
    grad_out_rows = dispatch(back_rows)
    grad_hidden = matmul_nt(grad_out_rows, down_w[0])
    unused_out, gelu_back = jax.vjp(jax.nn.gelu, hidden_pre)
    grad_pre = gelu_back(grad_hidden)[0].astype(jnp.bfloat16)
    grad_down = matmul_tn(hidden_b, grad_out_rows)
    grad_up = matmul_tn(rows_in, grad_pre)
    grad_in_rows = give_back(matmul_nt(grad_pre, up_w[0]), capacity)
    grad_normed = jnp.sum(pick_rows(grad_in_rows, slot_index).astype(jnp.float32), axis=1)
    grad_probs = jnp.sum(jnp.where(kept_pairs, grad_gates[..., None], 0.0), axis=1)
    grad_logits = gate_probs * (
        grad_probs - jnp.sum(gate_probs * grad_probs, axis=-1, keepdims=True)
    )
    grad_router = jnp.dot(normed_b.astype(jnp.float32).T, grad_logits, precision=highest)
    grad_normed = grad_normed + jnp.dot(grad_logits, router_w.T, precision=highest)
    grad_in, grad_gain = norm_backward(grad_normed, norm_gain, unit_rows, inverse)
    return (grad_stream + grad_in, grad_gain, grad_router, grad_up[None], grad_down[None])


def on_device(
    image_tokens,
    image_count,
    expert_routes,
    out_cotangent,
    norm_gains,
    attn_qkv,
    attn_proj,
    dense_up,
    dense_down,
    router_weight,
    expert_up,
    expert_down,
):
    stream = image_tokens.astype(jnp.float32)
    stream, early_attn = attention_forward(stream, norm_gains[0, 0], attn_qkv[0], attn_proj[0])
    stream, dense_state = dense_forward(stream, norm_gains[0, 1], dense_up, dense_down)
    stream, late_attn = attention_forward(stream, norm_gains[1, 0], attn_qkv[1], attn_proj[1])
    stream, expert_state = expert_forward(
        stream, norm_gains[1, 1], router_weight, expert_up, expert_down, expert_routes, image_count
    )
    grad_full = out_cotangent.astype(jnp.float32)
    gradient = grad_full
    gradient, gain_expert, grad_router, grad_ex_up, grad_ex_down = expert_backward(
        grad_full, gradient, norm_gains[1, 1], router_weight, expert_up, expert_down, expert_state
    )
    gradient, qkv_late, proj_late, gain_attn_late = attention_backward(
        gradient, norm_gains[1, 0], attn_qkv[1], attn_proj[1], late_attn
    )
    late_gains = jnp.stack([gain_attn_late, gain_expert])
    gradient, grad_dense_up, grad_dense_down, gain_dense = dense_backward(
        gradient, norm_gains[0, 1], dense_up, dense_down, dense_state
    )
    gradient, qkv_early, proj_early, gain_attn_early = attention_backward(
        gradient, norm_gains[0, 0], attn_qkv[0], attn_proj[0], early_attn
    )
    early_gains = jnp.stack([gain_attn_early, gain_dense])
    totals = (
        lax.psum(qkv_late.astype(jnp.bfloat16), "dp").astype(jnp.float32),
        lax.psum(proj_late.astype(jnp.bfloat16), "dp").astype(jnp.float32),
        lax.psum(late_gains.astype(jnp.bfloat16), "dp").astype(jnp.float32),
        lax.psum(grad_router.astype(jnp.bfloat16), "dp").astype(jnp.float32),
        lax.psum(qkv_early.astype(jnp.bfloat16), "dp").astype(jnp.float32),
        lax.psum(proj_early.astype(jnp.bfloat16), "dp").astype(jnp.float32),
        lax.psum(early_gains.astype(jnp.bfloat16), "dp").astype(jnp.float32),
        lax.psum(grad_dense_up.astype(jnp.bfloat16), "dp").astype(jnp.float32),
        lax.psum(grad_dense_down.astype(jnp.bfloat16), "dp").astype(jnp.float32),
    )
    late_sums = totals[:4]
    early_sums = totals[4:]
    gains_grad = jnp.stack([early_sums[2], late_sums[2]])
    qkv_grad = jnp.stack([early_sums[0], late_sums[0]])
    proj_grad = jnp.stack([early_sums[1], late_sums[1]])
    output_rows = stream.astype(jnp.bfloat16)
    return (
        output_rows,
        gradient,
        gains_grad,
        qkv_grad,
        proj_grad,
        early_sums[3],
        early_sums[4],
        late_sums[3],
        grad_ex_up,
        grad_ex_down,
    )


def solution(mesh):
    return jax.shard_map(
        on_device,
        mesh=mesh,
        in_specs=(
            P("dp", None),
            P("dp"),
            P("dp", None),
            P("dp", None),
            P(),
            P(None, None, None, "tensor"),
            P(None, "tensor", None),
            P(None, "tensor"),
            P("tensor", None),
            P(),
            P("dp", None, "tensor"),
            P("dp", "tensor", None),
        ),
        out_specs=(
            P("dp", None),
            P("dp", None),
            P(),
            P(None, None, None, "tensor"),
            P(None, "tensor", None),
            P(None, "tensor"),
            P("tensor", None),
            P(),
            P("dp", None, "tensor"),
            P("dp", "tensor", None),
        ),
        check_vma=False,
    )
```

profile of v0, /device:TPU:0, one launch (start us, length us, event | category | flops | bytes accessed | tf_op | source)
XLA Modules:
  0.0 1819.8 jit_solution(7835950379690443143)
XLA Ops:
  30.8 98.7 %all-reduce.15.cloned.1.call-done = f32[1576,768]{1,0:T(8,128)} async-done(((f32[1576,768]{1,0:T(8,128)}), f32[1576,768]{1,0:T(8,128)}) %all-reduce.15.cloned.1.call-update) | async-done | bytes 4841488 | tf_op jit(solution)/shard_map/psum | solution.py:31
  146.8 96.3 %all-reduce.17.cloned.1.call-done = f32[1576,768]{1,0:T(8,128)} async-done(((f32[1576,768]{1,0:T(8,128)}), f32[1576,768]{1,0:T(8,128)}) %all-reduce.17.cloned.1.call-update) | async-done | bytes 4841488 | tf_op jit(solution)/shard_map/psum | solution.py:31
  273.9 89.1 %all-reduce.19.cloned.1.call-done = f32[1576,768]{1,0:T(8,128)} async-done(((f32[1576,768]{1,0:T(8,128)}), f32[1576,768]{1,0:T(8,128)}) %all-reduce.19.cloned.1.call-update) | async-done | bytes 4841488 | tf_op jit(solution)/shard_map/psum | solution.py:31
  371.8 22.6 %broadcast_in_dim.42 = bf16[1576,2,768]{2,1,0:T(2,128)(2,1)} broadcast(bf16[1576,768]{1,0:T(8,128)(2,1)S(1)} %multiply_convert_fusion.5), dimensions={0,2} | broadcast | bytes 7262208 | tf_op jit(solution)/shard_map/broadcast_in_dim | solution.py:205
  394.4 10.9 reshape.326
  405.2 21.4 %scatter_custom_fusion = bf16[3169,768]{1,0:T(8,128)(2,1)} fusion(s32[3152]{0:T(1024)S(1)} %fusion.144, bf16[3152,768]{1,0:T(8,128)(2,1)} %reshape.326, bf16[]{:T(256)} %constant.69.clone.1), kind=kCustom, calls=%fused_computation.100 | custom fusion | bytes 4868096 | tf_op jit(solution)/shard_map/scatter | solution.py:174
  442.7 19.7 %mul.414 = f32[1576,2,768]{2,1,0:T(2,128)} broadcast(bf16[1576,768]{1,0:T(8,128)(2,1)} %param.15), dimensions={0,2} | broadcast | bytes 12103680 | tf_op jit(solution)/shard_map/mul | solution.py:247
  462.3 12.5 mul.415
  479.4 32.3 %scatter_custom_fusion.1 = bf16[3169,768]{1,0:T(8,128)(2,1)} fusion(s32[3152]{0:T(1024)S(1)} %fusion.144, f32[3152,768]{1,0:T(8,128)} %mul.415, f32[3152]{0:T(1024)S(1)} %mul.412, bf16[]{:T(256)} %constant.69.clone.1), kind=kCustom, calls=%fused_computation.54 | custom fusion | flops 4841472 | bytes 14566914 | tf_op jit(solution)/shard_map/scatter | solution.py:174
  522.1 29.2 %all-to-all-done = bf16[8,396,768]{2,1,0:T(8,128)(2,1)} async-done(((bf16[8,396,768]{2,1,0:T(8,128)(2,1)}), bf16[8,396,768]{2,1,0:T(8,128)(2,1)}, u32[]{:S(2)}, u32[]{:S(2)}) %all-to-all-start) | async-done | bytes 4866080 | tf_op jit(solution)/shard_map/all_to_all | solution.py:159
  571.2 7.6 convolution_convert_fusion.1
  578.8 85.0 %all-to-all-done.2 = bf16[8,396,768]{2,1,0:T(8,128)(2,1)} async-done(((bf16[8,396,768]{2,1,0:T(8,128)(2,1)}), bf16[8,396,768]{2,1,0:T(8,128)(2,1)}, u32[]{:S(2)}, u32[]{:S(2)}) %all-to-all-start.2) | async-done | bytes 4866080 | tf_op jit(solution)/shard_map/all_to_all | solution.py:159
  669.2 12.2 fusion.6
  700.1 175.2 %all-reduce.29.cloned.1.call-done = (bf16[8,396,768]{2,1,0:T(8,128)(2,1)}, bf16[8,396,768]{2,1,0:T(8,128)(2,1)}) async-done(((bf16[8,396,768]{2,1,0:T(8,128)(2,1)}, bf16[8,396,768]{2,1,0:T(8,128)(2,1)}), (bf16[8,396,768]{2,1,0:T(8,128)(2,1)}, bf16[8,396,768]{2,1,0:T(8,128)(2,1)})) %all-reduce.29.cloned.1.call-update) | async-done | bytes 9732112 | tf_op jit(solution)/shard_map/psum | solution.py:165
  875.4 114.3 %all_to_all.20 = bf16[8,396,768]{2,1,0:T(8,128)(2,1)} all-to-all(bf16[8,396,768]{2,1,0:T(8,128)(2,1)} %get-tuple-element.38), channel_id=1, replica_groups=mesh['dp'=8,'tensor'=4] {'dp'}, dimensions={0} | all-to-all | bytes 9732096 | tf_op jit(solution)/shard_map/all_to_all | solution.py:166
  1009.9 91.9 %all-to-all-done.1 = bf16[8,396,768]{2,1,0:T(8,128)(2,1)} async-done(((bf16[8,396,768]{2,1,0:T(8,128)(2,1)}), bf16[8,396,768]{2,1,0:T(8,128)(2,1)}, u32[]{:S(2)}, u32[]{:S(2)}) %all-to-all-start.1) | async-done | bytes 4866080 | tf_op jit(solution)/shard_map/all_to_all | solution.py:166
  1112.1 15.9 gather_fusion.1
  1128.0 15.9 gather_fusion
  1144.0 11.5 reshape.342
  1155.4 24.9 %multiply_reduce_fusion = (f32[1576,2]{1,0:T(8,128)S(1)}, f32[1576,768]{1,0:T(8,128)}) fusion(f32[1576,2,768]{2,1,0:T(2,128)} %reshape.342, f32[1576,768]{1,0:T(8,128)} %convert_element_type.182, f32[1576,2]{1,0:T(8,128)S(1)} %copy.173), kind=kLoop, calls=%fused_computation.14 | loop fusion | flops 8469424 | bytes 19391104 | tf_op jit(solution)/shard_map/reduce_sum | solution.py:246
  1180.7 11.5 reshape.343
  1192.2 45.1 %reduce_sum.302 = f32[1576,768]{1,0:T(8,128)} reduce(f32[1576,2,768]{2,1,0:T(2,128)} %reshape.343, f32[]{:T(128)} %constant.26.clone.1), dimensions={1}, to_apply=%region_26.27 | reduce | flops 1210368 | bytes 14524420 | tf_op jit(solution)/shard_map/reduce_sum | solution.py:258
  1237.4 10.2 multiply_reduce_fusion.4
  1279.8 95.0 %all-reduce.21.cloned.1.call-done = f32[1576,768]{1,0:T(8,128)} async-done(((f32[1576,768]{1,0:T(8,128)}), f32[1576,768]{1,0:T(8,128)}) %all-reduce.21.cloned.1.call-update) | async-done | bytes 4841488 | tf_op jit(solution)/shard_map/psum | solution.py:31
  1402.8 89.4 %all-reduce.23.cloned.1.call-done = f32[1576,768]{1,0:T(8,128)} async-done(((f32[1576,768]{1,0:T(8,128)}), f32[1576,768]{1,0:T(8,128)}) %all-reduce.23.cloned.1.call-update) | async-done | bytes 4841488 | tf_op jit(solution)/shard_map/psum | solution.py:31
  1541.0 7.9 convolution_convert_fusion.4
  1554.6 9.7 convolution_bitcast_fusion.3
  1564.3 10.5 convolution_bitcast_fusion.2
  1576.0 50.0 %all-reduce.25.cloned.1.call-done = f32[1576,768]{1,0:T(8,128)} async-done(((f32[1576,768]{1,0:T(8,128)}), f32[1576,768]{1,0:T(8,128)}) %all-reduce.25.cloned.1.call-update) | async-done | bytes 4841488 | tf_op jit(solution)/shard_map/psum | solution.py:31
  1631.1 38.9 %all-reduce.3 = (bf16[1,2,768]{2,1,0:T(2,128)(2,1)S(1)}, bf16[1,2,768]{2,1,0:T(2,128)(2,1)S(1)}, bf16[768,8]{0,1:T(8,128)(2,1)S(1)}) all-reduce(bf16[1,2,768]{2,1,0:T(2,128)(2,1)S(1)} %maximum_bitcast_fusion.1, bf16[1,2,768]{2,1,0:T(2,128)(2,1)S(1)} %maximum_bitcast_fusion, ...), channel_id=1, replica_groups=mesh['dp'=8,'tensor'=4] {'dp'}, use_global_device_ids=true, to_apply=%region_48.49 | all-reduce | flops 9216 | bytes 36864 | tf_op jit(solution)/shard_map/psum | solution.py:309
  1671.2 6.9 fusion.17
  1678.1 125.6 %all-reduce.27.cloned.1.call-done = (bf16[1,3,768,192]{2,3,1,0:T(8,128)(2,1)}, bf16[1,3,768,192]{2,3,1,0:T(8,128)(2,1)}, bf16[1,192,768]{2,1,0:T(8,128)(2,1)}, b...) async-done(((bf16[1,3,768,192]{2,3,1,0:T(8,128)(2,1)}, bf16[1,3,768,192]{2,3,1,0:T(8,128)(2,1)}, bf16[1,192,768]{2,1,0:T(8,128)(2,1)}, ...) | async-done | bytes 4718608 | tf_op jit(solution)/shard_map/psum | solution.py:307
  (393 shorter events, 315.1 us)
Async XLA Ops:
  7.2 564.0 %copy-start = (bf16[1,768,768]{2,1,0:T(8,128)(2,1)S(1)}, bf16[1,768,768]{2,1,0:T(8,128)(2,1)}, u32[]{:S(2)}) copy-start(bf16[1,768,768]{2,1,0:T(8,128)(2,1)} %param.23) | copy-start | bytes 3538948
  7.2 122.3 %all-reduce.15.cloned.1.call-start = ((), (), s32[]{:S(2)}) async-start(), calls=%async_computation.4 | async-start | bytes 9682944 | tf_op jit(solution)/shard_map/psum | solution.py:31
  12.2 121.8 %copy-start.73 = (f32[768]{0:T(1024)}, f32[768]{0:T(1024)S(1)}, u32[]{:S(2)}) copy-start(f32[768]{0:T(1024)S(1)} %get-tuple-element.25) | copy-start | bytes 9220
  12.2 236.1 %copy-start.79 = (f32[768]{0:T(1024)}, f32[768]{0:T(1024)S(1)}, u32[]{:S(2)}) copy-start(f32[768]{0:T(1024)S(1)} %get-tuple-element.27) | copy-start | bytes 9220
  12.2 356.0 %copy-start.75 = (f32[768]{0:T(1024)}, f32[768]{0:T(1024)S(1)}, u32[]{:S(2)}) copy-start(f32[768]{0:T(1024)S(1)} %get-tuple-element.24) | copy-start | bytes 9220
  30.6 212.5 %all-reduce.17.cloned.1.call-start = ((), (), s32[]{:S(2)}) async-start(), calls=%async_computation.5 | async-start | bytes 9682944 | tf_op jit(solution)/shard_map/psum | solution.py:31
  146.8 216.3 %all-reduce.19.cloned.1.call-start = ((), (), s32[]{:S(2)}) async-start(), calls=%async_computation.6 | async-start | bytes 9682944 | tf_op jit(solution)/shard_map/psum | solution.py:31
  436.9 114.3 %all-to-all-start = ((bf16[8,396,768]{2,1,0:T(8,128)(2,1)}), bf16[8,396,768]{2,1,0:T(8,128)(2,1)}, u32[]{:S(2)}, u32[]{:S(2)}) async-start(bf16[8,396,768]{2,1,0:T(8,128)(2,1)} %reshape.295), calls=%async_computation | async-start | bytes 9830400 | tf_op jit(solution)/shard_map/all_to_all | solution.py:159
  462.3 12.5 copy-start.68
  551.2 112.6 %all-to-all-start.2 = ((bf16[8,396,768]{2,1,0:T(8,128)(2,1)}), bf16[8,396,768]{2,1,0:T(8,128)(2,1)}, u32[]{:S(2)}, u32[]{:S(2)}) async-start(bf16[8,396,768]{2,1,0:T(8,128)(2,1)} %reshape.299), calls=%async_computation.2 | async-start | bytes 9830400 | tf_op jit(solution)/shard_map/all_to_all | solution.py:159
  555.9 319.5 %all-reduce.29.cloned.1.call-start = ((), (), s32[]{:S(2)}) async-start(), calls=%async_computation.11 | async-start | bytes 19660800 | tf_op jit(solution)/shard_map/psum | solution.py:165
  989.7 112.1 %all-to-all-start.1 = ((bf16[8,396,768]{2,1,0:T(8,128)(2,1)}), bf16[8,396,768]{2,1,0:T(8,128)(2,1)}, u32[]{:S(2)}, u32[]{:S(2)}) async-start(bf16[8,396,768]{2,1,0:T(8,128)(2,1)} %get-tuple-element.37), calls=%async_computation.1 | async-start | bytes 9830400 | tf_op jit(solution)/shard_map/all_to_all | solution.py:166
  994.3 380.4 %all-reduce.21.cloned.1.call-start = ((), (), s32[]{:S(2)}) async-start(), calls=%async_computation.7 | async-start | bytes 9682944 | tf_op jit(solution)/shard_map/psum | solution.py:31
  1192.2 45.2 %copy-start.53 = (f32[1576]{0:T(1024)S(1)}, f32[1576]{0:T(1024)}, u32[]{:S(2)}) copy-start(f32[1576]{0:T(1024)} %copy-done.52) | copy-start | bytes 18916
  1192.2 45.2 %copy-start.57 = (f32[1576]{0:T(1024)S(1)}, f32[1576]{0:T(1024)}, u32[]{:S(2)}) copy-start(f32[1576]{0:T(1024)} %copy-done.56) | copy-start | bytes 18916
  1192.2 45.2 %copy-start.76 = (f32[768]{0:T(1024)S(1)}, f32[768]{0:T(1024)}, u32[]{:S(2)}) copy-start(f32[768]{0:T(1024)} %copy-done.75) | copy-start | bytes 9220
  1192.2 55.4 %slice-start.4 = ((s8[4841472]{0:T(1024)(128)(4,1)}), s8[647168]{0:T(1024)(128)(4,1)S(1)}, s32[]{:S(2)}) async-start(s8[4841472]{0:T(1024)(128)(4,1)} %bitcast.195), calls=%async_computation.16 | async-start | bytes 1294336
  1237.3 10.3 slice-start.5
  1237.3 10.3 copy-start.13
  1279.7 95.1 %copy-start.61 = (f32[1576]{0:T(1024)S(1)}, f32[1576]{0:T(1024)}, u32[]{:S(2)}) copy-start(f32[1576]{0:T(1024)} %copy-done.60) | copy-start | bytes 18916
  1279.7 95.1 %copy-start.72 = (f32[1576]{0:T(1024)S(1)}, f32[1576]{0:T(1024)}, u32[]{:S(2)}) copy-start(f32[1576]{0:T(1024)} %copy-done.71) | copy-start | bytes 18916
  1279.7 95.1 %copy-start.80 = (f32[768]{0:T(1024)S(1)}, f32[768]{0:T(1024)}, u32[]{:S(2)}) copy-start(f32[768]{0:T(1024)} %copy-done.79) | copy-start | bytes 9220
  1279.7 212.5 %all-reduce.23.cloned.1.call-start = ((), (), s32[]{:S(2)}) async-start(), calls=%async_computation.8 | async-start | bytes 9682944 | tf_op jit(solution)/shard_map/psum | solution.py:31
  1374.8 10.6 slice-start.10
  1395.8 230.1 %all-reduce.25.cloned.1.call-start = ((), (), s32[]{:S(2)}) async-start(), calls=%async_computation.9 | async-start | bytes 9682944 | tf_op jit(solution)/shard_map/psum | solution.py:31
  1397.3 94.8 %copy-start.55 = (f32[1576]{0:T(1024)S(1)}, f32[1576]{0:T(1024)}, u32[]{:S(2)}) copy-start(f32[1576]{0:T(1024)} %copy-done.54) | copy-start | bytes 18916
  1397.3 94.8 %copy-start.67 = (f32[1576]{0:T(1024)S(1)}, f32[1576]{0:T(1024)}, u32[]{:S(2)}) copy-start(f32[1576]{0:T(1024)} %copy-done.66) | copy-start | bytes 18916
  1397.3 94.8 %copy-start.74 = (f32[768]{0:T(1024)S(1)}, f32[768]{0:T(1024)}, u32[]{:S(2)}) copy-start(f32[768]{0:T(1024)} %copy-done.73) | copy-start | bytes 9220
  1529.5 274.1 %all-reduce.27.cloned.1.call-start = ((), (), s32[]{:S(2)}) async-start(), calls=%async_computation.10 | async-start | bytes 9437184 | tf_op jit(solution)/shard_map/psum | solution.py:307
  1534.4 14.5 slice-start.6
  1551.3 13.0 slice-start.8
  1564.3 10.6 copy-start.12
  (82 other events, 308.9 us)
Sparse Core Ops, SparseCore 0:
  30.7 98.7 all-reduce.14
  146.9 96.1 all-reduce.16
  266.8 96.2 all-reduce.18
  700.3 175.0 all-reduce.28
  1279.8 94.8 all-reduce.20
  1395.9 96.1 all-reduce.22
  1529.6 96.2 all-reduce.24
  1631.4 172.2 all-reduce.26
where the time goes:
time: 1830 us; the launch traced here: 1820 us
  waiting for transfers between devices  1030 us (56%)
  local copies, waits for them, and re-layouts  264 us (14%)
  other arithmetic  185 us (10%)
  matrix products  160 us (9%)
  blocking collectives  153 us (8%)
    psum x6, waiting for transfers between devices, tensor_total(): return lax.psum(term_rows(0, tokens), 'tensor')  519 us
    psum x1, waiting for transfers between devices, give_back(): summed_rows = lax.psum(partial_out.astype(jnp.bfloat16), 'tensor')  175 us
    psum x1, waiting for transfers between devices, on_device(): lax.psum(qkv_late.astype(jnp.bfloat16), 'dp').astype(jnp.float32)  126 us
    all_to_all x1, blocking collectives, give_back(): lax.all_to_all(summed_rows.reshape(sources, capacity, -1), 'dp', split_ax...  114 us
    all_to_all x2, waiting for transfers between devices, dispatch(): lax.all_to_all(send_rows, 'dp', split_axis=0, concat_axis=0, tiled=True)  114 us
    all_to_all x1, waiting for transfers between devices, give_back(): lax.all_to_all(summed_rows.reshape(sources, capacity, -1), 'dp', split_ax...  91.9 us
    reduce_sum x1, other arithmetic, expert_backward(): jnp.sum(pick_rows(grad_in_rows, slot_index).astype(jnp.float32), axis=1)  45.1 us
    dot_general x6, matrix products, matmul_tn(): lax.dot_general(left_side, right_side, (((0,), (0,)), ((), ())), preferre...  40.1 us
  transfers between devices with their start and end apart: 11, of which 11 were waited for; matrix products, arithmetic and copies ran while one was open for 10% of the time, Pallas kernels for 0%

commit v1 on v0

v1 whole, which is shorter than its diff:
```python
import jax
import jax.numpy as jnp
from jax import lax
from jax.sharding import PartitionSpec as P

HD = 64
SEQ = 197
PAD = 200

epsilon = 1e-06
highest = lax.Precision.HIGHEST
bf16 = jnp.bfloat16
f32 = jnp.float32


def matmul(left_side, right_side):
    return jnp.dot(left_side, right_side, preferred_element_type=f32)


def matmul_tn(left_side, right_side):
    return lax.dot_general(
        left_side, right_side, (((0,), (0,)), ((), ())), preferred_element_type=f32
    )


def matmul_nt(left_side, right_side):
    return lax.dot_general(
        left_side, right_side, (((1,), (1,)), ((), ())), preferred_element_type=f32
    )


def flip(values, mask):
    ranks = lax.axis_size("tensor")
    return lax.ppermute(values, "tensor", [(i, i ^ mask) for i in range(ranks)])


def after(values, earlier):
    return lax.optimization_barrier((values, earlier))[0]


def far(own, earlier=None):
    if earlier is not None:
        own = after(own, earlier)
    return flip(own, 2)


def near(own, far_own):
    return [own, flip(own, 1), far_own, flip(far_own, 1)]


def gather(own):
    return near(own, far(own))


def add_rounded(left_side, right_side):
    return (left_side.astype(f32) + right_side.astype(f32)).astype(bf16)


def scatter_sum(parts):
    mine = add_rounded(parts[0], flip(parts[1], 1))
    other = add_rounded(parts[2], flip(parts[3], 1))
    return add_rounded(mine, flip(other, 2))


def norm_forward(values, norm_gain):
    centered = values - jnp.mean(values, axis=-1, keepdims=True)
    inverse = lax.rsqrt(jnp.mean(centered * centered, axis=-1, keepdims=True) + epsilon)
    unit_rows = centered * inverse
    return (unit_rows * norm_gain, unit_rows, inverse)


def norm_backward(grad_out, norm_gain, unit_rows, inverse):
    grad_unit = grad_out * norm_gain
    grad_in = inverse * (
        grad_unit
        - jnp.mean(grad_unit, axis=-1, keepdims=True)
        - unit_rows * jnp.mean(grad_unit * unit_rows, axis=-1, keepdims=True)
    )
    return (grad_in, jnp.sum(grad_out * unit_rows, axis=0))


def masked_scores(queries, key_rows):
    scores = jnp.einsum(
        "ishd,ithd->ihst", queries, key_rows, preferred_element_type=f32
    ) * HD ** (-0.5)
    return jnp.where(jnp.arange(PAD) < SEQ, scores, -1e30)


def attention_forward(stream, norm_gain, qkv_w, proj_w):
    normed, unit_rows, inverse = norm_forward(stream, norm_gain)
    normed_b = normed.astype(bf16)
    tokens = normed_b.shape[0]
    projected = jnp.einsum("td,jcd->jtc", normed_b, qkv_w, preferred_element_type=f32)
    rounded = projected.astype(bf16).reshape(3, tokens // PAD, PAD, -1, HD)
    queries, key_rows, value_rows = (rounded[0], rounded[1], rounded[2])
    scores = masked_scores(queries, key_rows)
    row_peak = jnp.max(scores, axis=-1, keepdims=True)
    weights = jnp.exp(scores - row_peak)
    row_total = jnp.sum(weights, axis=-1, keepdims=True)
    log_total = row_peak + jnp.log(row_total)
    weights_b = (weights / row_total).astype(bf16)
    context = jnp.einsum("ihst,ithd->ishd", weights_b, value_rows, preferred_element_type=f32)
    context = context.astype(bf16).reshape(tokens, -1)
    return (
        stream + matmul(context, proj_w),
        (unit_rows, inverse, normed_b, queries, key_rows, value_rows, log_total, context),
    )


def attention_backward(grad_stream, norm_gain, qkv_w, proj_w, saved_state):
    unit_rows, inverse, normed_b, queries, key_rows, value_rows, log_total, context = saved_state
    tokens = normed_b.shape[0]
    grad_branch = grad_stream.astype(bf16)
    grad_proj = matmul_tn(context, grad_branch)
    grad_context = matmul_nt(grad_branch, proj_w).astype(bf16).reshape(queries.shape)
    probs_again = jnp.exp(masked_scores(queries, key_rows) - log_total)
    grad_weights = jnp.einsum(
        "ishd,ithd->ihst", grad_context, value_rows, preferred_element_type=f32
    )
    grad_values = jnp.einsum(
        "ihst,ishd->ithd", probs_again.astype(bf16), grad_context, preferred_element_type=f32
    )
    grad_scores = probs_again * (
        grad_weights - jnp.sum(probs_again * grad_weights, axis=-1, keepdims=True)
    )
    grad_scores = grad_scores.astype(bf16)
    grad_queries = jnp.einsum(
        "ihst,ithd->ishd", grad_scores, key_rows, preferred_element_type=f32
    ) * HD ** (-0.5)
    grad_keys = jnp.einsum(
        "ihst,ishd->ithd", grad_scores, queries, preferred_element_type=f32
    ) * HD ** (-0.5)
    stacked = (
        jnp.stack([grad_queries, grad_keys, grad_values]).astype(bf16).reshape(3, tokens, -1)
    )
    grad_qkv = jnp.einsum("jtc,td->jcd", stacked, normed_b, preferred_element_type=f32)
    grad_normed = jnp.einsum("jtc,jcd->td", stacked, qkv_w, preferred_element_type=f32)
    grad_in, grad_gain = norm_backward(grad_normed, norm_gain, unit_rows, inverse)
    return (grad_stream + grad_in, grad_qkv.astype(bf16), grad_proj.astype(bf16), grad_gain)


def dense_forward(stream, norm_gain, up_w, down_w):
    normed, unit_rows, inverse = norm_forward(stream, norm_gain)
    normed_b = normed.astype(bf16)
    hidden_pre = matmul(normed_b, up_w)
    hidden_b = jax.nn.gelu(hidden_pre).astype(bf16)
    return (
        stream + matmul(hidden_b, down_w),
        (unit_rows, inverse, normed_b, hidden_pre, hidden_b),
    )


def dense_backward(grad_stream, norm_gain, up_w, down_w, saved_state):
    unit_rows, inverse, normed_b, hidden_pre, hidden_b = saved_state
    grad_branch = grad_stream.astype(bf16)
    grad_down = matmul_tn(hidden_b, grad_branch)
    unused_out, gelu_back = jax.vjp(jax.nn.gelu, hidden_pre)
    grad_pre = gelu_back(matmul_nt(grad_branch, down_w))[0].astype(bf16)
    grad_up = matmul_tn(normed_b, grad_pre)
    grad_normed = matmul_nt(grad_pre, up_w)
    grad_in, grad_gain = norm_backward(grad_normed, norm_gain, unit_rows, inverse)
    return (grad_stream + grad_in, grad_up.astype(bf16), grad_down.astype(bf16), grad_gain)


def row_parts(values, axis):
    return jnp.split(values, lax.axis_size("tensor"), axis=axis)


def to_padded(rows):
    images = rows.shape[0] // SEQ
    padded = jnp.pad(rows.reshape(images, SEQ, -1), ((0, 0), (0, PAD - SEQ), (0, 0)))
    return padded.reshape(images * PAD, -1)


def in_order(blocks, me):
    ordered = [lax.select_n(me ^ a, *blocks) for a in range(len(blocks))]
    rows = jnp.stack(ordered).reshape(-1, PAD, blocks[0].shape[1])[:, :SEQ]
    return rows.reshape(-1, blocks[0].shape[1])


def all_to_all(rows):
    sources = lax.axis_size("dp")
    split_rows = rows.reshape(sources, -1, rows.shape[1])
    arrived = lax.all_to_all(split_rows, "dp", split_axis=0, concat_axis=0, tiled=True)
    return arrived.reshape(rows.shape)


def slots_of(routes, live_count):
    tokens = routes.shape[0]
    experts = lax.axis_size("dp")
    live_rows = jnp.arange(tokens, dtype=jnp.int32) // SEQ < live_count[0]
    chosen = routes[..., None] == jnp.arange(experts, dtype=jnp.int32)
    kept = (chosen & live_rows[:, None, None]).astype(jnp.int32).reshape(tokens * 2, experts)
    rank = jnp.sum((jnp.cumsum(kept, axis=0) - kept) * kept, axis=-1).reshape(tokens, 2)
    return jnp.where(live_rows[:, None], rank, -1)


def on_device(
    image_tokens,
    image_count,
    expert_routes,
    out_cotangent,
    norm_gains,
    attn_qkv,
    attn_proj,
    dense_up,
    dense_down,
    router_weight,
    expert_up,
    expert_down,
):
    ranks = lax.axis_size("tensor")
    experts = lax.axis_size("dp")
    me = lax.axis_index("tensor")
    tokens, width = image_tokens.shape
    own_rows = tokens // ranks
    block = own_rows // SEQ * PAD
    order = [me ^ k for k in range(ranks)]

    def own_of(whole):
        return lax.dynamic_slice_in_dim(whole, me * own_rows, own_rows, 0)

    qkv_t = jnp.swapaxes(attn_qkv, 2, 3)
    far_qkv0 = far(qkv_t[0])
    far_proj0 = far(attn_proj[0], far_qkv0)
    far_up = far(dense_up, far_proj0)
    far_down = far(dense_down, far_up)
    far_qkv1 = far(qkv_t[1], far_down)
    far_proj1 = far(attn_proj[1], far_qkv1)
    qkv0 = jnp.concatenate(near(qkv_t[0], far_qkv0), axis=1)
    proj0 = jnp.concatenate(near(attn_proj[0], far_proj0), axis=0)
    up_w = jnp.concatenate(near(dense_up, far_up), axis=1)
    down_w = jnp.concatenate(near(dense_down, far_down), axis=0)
    qkv1 = jnp.concatenate(near(qkv_t[1], far_qkv1), axis=1)
    proj1 = jnp.concatenate(near(attn_proj[1], far_proj1), axis=0)

    capacity = (2 * tokens + experts - 1) // experts + 2
    quota = -(-capacity // ranks)
    room = -(-quota // 8) * 8
    slots = experts * room
    rank = slots_of(expert_routes, image_count)
    holder = jnp.where(rank < 0, -1, rank // quota)
    place = expert_routes * room + rank - holder * quota
    mine = jnp.where(holder == me, place, -1)

    def blocked(values):
        images = tokens // SEQ
        padded = jnp.pad(
            values.T.reshape(2, images, SEQ), ((0, 0), (0, 0), (0, PAD - SEQ)), constant_values=-1
        ).reshape(2, ranks, block)
        return jnp.stack([padded[:, one] for one in order], axis=1)

    place_rel = blocked(mine).reshape(2, ranks * block)
    slot_ids = jnp.arange(slots, dtype=jnp.int32)[:, None]
    first = slot_ids == place_rel[0]
    second = slot_ids == place_rel[1]
    pick = (first | second).astype(bf16)
    pick_whole = ((slot_ids == mine[:, 0]) | (slot_ids == mine[:, 1])).astype(bf16)

    stream0 = to_padded(own_of(image_tokens)).astype(f32)
    grad_out = to_padded(own_of(out_cotangent)).astype(f32)
    stream1, attn0_state = attention_forward(stream0, norm_gains[0, 0], qkv0, proj0)
    stream2, dense_state = dense_forward(stream1, norm_gains[0, 1], up_w, down_w)
    stream3, attn1_state = attention_forward(stream2, norm_gains[1, 0], qkv1, proj1)

    normed, unit_rows, inverse = norm_forward(stream3, norm_gains[1, 1])
    normed_b = normed.astype(bf16)
    far_normed = far(normed_b, far_proj1)
    normed_all = jnp.concatenate(near(normed_b, far_normed), axis=0)
    far_ex_up = far(expert_up[0], far_normed)
    far_ex_down = far(expert_down[0], far_ex_up)
    ex_up = jnp.concatenate(near(expert_up[0], far_ex_up), axis=1)
    ex_down = jnp.concatenate(near(expert_down[0], far_ex_down), axis=0)

    rows_in = all_to_all(matmul(pick, normed_all).astype(bf16))
    logits = jnp.dot(normed_all.astype(f32), router_weight, precision=highest)
    gate_all = jax.nn.softmax(logits, axis=-1)
    gate_probs = gate_all[:block]
    routes_rel = blocked(expert_routes).reshape(2, ranks * block)
    expert_ids = jnp.arange(experts, dtype=jnp.int32)
    chosen_rel = routes_rel[..., None] == expert_ids
    gates = jnp.sum(jnp.where(chosen_rel, gate_all[None], 0.0), axis=-1)
    gate_slot = jnp.sum(
        jnp.where(first, gates[0], 0.0) + jnp.where(second, gates[1], 0.0), axis=1
    )[:, None]
    cot_slot = matmul(pick_whole, out_cotangent)
    grad_rows = all_to_all((gate_slot * cot_slot).astype(bf16))

    hidden_pre = matmul(rows_in, ex_up)
    hidden_b = jax.nn.gelu(hidden_pre).astype(bf16)
    rows_out = all_to_all(matmul(hidden_b, ex_down).astype(bf16))
    unused_out, gelu_back = jax.vjp(jax.nn.gelu, hidden_pre)
    grad_pre = gelu_back(matmul_nt(grad_rows, ex_down))[0].astype(bf16)
    grad_back = all_to_all(matmul_nt(grad_pre, ex_up).astype(bf16))
    grad_ex_down = scatter_sum(row_parts(matmul_tn(hidden_b, grad_rows).astype(bf16), 0))
    grad_ex_up = scatter_sum(row_parts(matmul_tn(rows_in, grad_pre).astype(bf16), 1))

    out_f = rows_out.astype(f32)
    gate_grad_slot = jnp.sum(cot_slot * out_f, axis=1)
    branch = matmul_tn(pick, (gate_slot * out_f).astype(bf16)).astype(bf16)
    stream4 = stream3 + scatter_sum(row_parts(branch, 0)).astype(f32)
    block_output = in_order(gather(stream4.astype(bf16)), me)

    own_holder = blocked(holder)[:, 0]
    own_place = blocked(place)[:, 0]
    own_routes = blocked(expert_routes)[:, 0]
    grad_gates = 0.0
    for one, values in zip(order, gather(gate_grad_slot)):
        here = jnp.where(own_holder == one, own_place, -1)
        found = here[..., None] == jnp.arange(slots, dtype=jnp.int32)
        grad_gates = grad_gates + jnp.sum(jnp.where(found, values, 0.0), axis=-1)
    grad_probs = jnp.sum(
        jnp.where(own_routes[..., None] == expert_ids, grad_gates[..., None], 0.0), axis=0
    )
    grad_logits = gate_probs * (
        grad_probs - jnp.sum(gate_probs * grad_probs, axis=-1, keepdims=True)
    )
    grad_router = jnp.dot(normed_b.astype(f32).T, grad_logits, precision=highest)
    grad_branch = matmul_tn(pick, grad_back).astype(bf16)
    grad_normed = scatter_sum(row_parts(grad_branch, 0)).astype(f32)
    grad_normed = grad_normed + jnp.dot(grad_logits, router_weight.T, precision=highest)
    grad_in, gain_expert = norm_backward(grad_normed, norm_gains[1, 1], unit_rows, inverse)
    grad3 = grad_out + grad_in

    def small_sum(values):
        values = values.astype(bf16)
        values = add_rounded(values, flip(values, 1))
        return add_rounded(values, flip(values, 2))

    def total(*parts):
        return lax.psum(jnp.concatenate(parts, axis=0), "dp").astype(f32)

    def qkv_rows(grad_qkv):
        own = scatter_sum(row_parts(grad_qkv, 1))
        return own.reshape(-1, width)

    grad2, grad_qkv1, grad_proj1, gain_attn1 = attention_backward(
        grad3, norm_gains[1, 0], qkv1, proj1, attn1_state
    )
    smalls1 = small_sum(
        jnp.concatenate([gain_attn1[None], gain_expert[None], grad_router.T], axis=0)
    )
    sums1 = total(qkv_rows(grad_qkv1), scatter_sum(row_parts(grad_proj1, 0)), smalls1)
    grad1, grad_up, grad_down, gain_dense = dense_backward(
        grad2, norm_gains[0, 1], up_w, down_w, dense_state
    )
    down_part = scatter_sum(row_parts(grad_down, 0))
    up_part = scatter_sum(row_parts(grad_up, 1))
    sums_dense = total(after(up_part, sums1), down_part)
    grad0, grad_qkv0, grad_proj0, gain_attn0 = attention_backward(
        grad1, norm_gains[0, 0], qkv0, proj0, attn0_state
    )
    smalls0 = small_sum(jnp.concatenate([gain_attn0[None], gain_dense[None]], axis=0))
    proj_part0 = scatter_sum(row_parts(grad_proj0, 0))
    sums0 = total(after(qkv_rows(grad_qkv0), sums_dense), proj_part0, smalls0)
    input_grad = in_order(gather(grad0.astype(bf16)), me).astype(f32)

    columns = attn_qkv.shape[3]
    grad_qkv = jnp.stack(
        [jnp.swapaxes(sums[: 3 * columns].reshape(3, columns, width), 1, 2) for sums in (sums0, sums1)]
    )
    grad_proj = jnp.stack([sums[3 * columns : 4 * columns] for sums in (sums0, sums1)])
    grad_gains = jnp.stack(
        [sums[4 * columns : 4 * columns + 2] for sums in (sums0, sums1)]
    )
    router_grad = sums1[4 * columns + 2 :].T
    return (
        block_output,
        input_grad,
        grad_gains,
        grad_qkv,
        grad_proj,
        sums_dense[:width],
        sums_dense[width:],
        router_grad,
        grad_ex_up.astype(f32)[None],
        grad_ex_down.astype(f32)[None],
    )


def solution(mesh):
    return jax.shard_map(
        on_device,
        mesh=mesh,
        in_specs=(
            P("dp", None),
            P("dp"),
            P("dp", None),
            P("dp", None),
            P(),
            P(None, None, None, "tensor"),
            P(None, "tensor", None),
            P(None, "tensor"),
            P("tensor", None),
            P(),
            P("dp", None, "tensor"),
            P("dp", "tensor", None),
        ),
        out_specs=(
            P("dp", None),
            P("dp", None),
            P(),
            P(None, None, None, "tensor"),
            P(None, "tensor", None),
            P(None, "tensor"),
            P("tensor", None),
            P(),
            P("dp", None, "tensor"),
            P("dp", "tensor", None),
        ),
        check_vma=False,
    )
```

time: 1830 us -> 920 us (0.50)
  waiting for transfers between devices: 1030 us -> 448 us
  blocking collectives: 153 us -> 0 us
  local copies, waits for them, and re-layouts: 264 us -> 136 us
  other arithmetic: 185 us -> 64.5 us
  starting transfers between devices: 15.6 us -> 63.2 us
  matrix products: 160 us -> 182 us
    psum x8 -> x3, waiting for transfers between devices: 819 us -> 167 us  [total(): return lax.psum(jnp.concatenate(parts, axis=0), 'dp').astype(f32)]
    ppermute x0 -> x70, waiting for transfers between devices: none -> 225 us  [flip(): return lax.ppermute(values, 'tensor', [(i, i ^ mask) for i in range(ranks)])]
    all_to_all x3 -> x4, waiting for transfers between devices: 206 us -> 56 us  [all_to_all(): lax.all_to_all(split_rows, 'dp', split_axis=0, concat_axis=0, tiled=True)]
    all_to_all x1 -> x0, blocking collectives: 114 us -> none  [give_back(): lax.all_to_all(summed_rows.reshape(sources, capacity, -1), 'dp', split_ax...]
    reduce_sum x10, other arithmetic: 86.8 us -> 3.72 us  [the longest x4 2.14 us: on_device(): grad_gates = grad_gates + jnp.sum(jnp.where(found, values, 0.0), axis=-1)]
    reshape x16 -> x19, local copies, waits for them, and re-layouts: 60.3 us -> 18 us  [the longest x4 8.5 us: attention_backward(): matmul_nt(grad_branch, proj_w).astype(bf16).reshape(queries.shape)]
    ppermute x0 -> x70, starting transfers between devices: none -> 41.5 us  [flip(): return lax.ppermute(values, 'tensor', [(i, i ^ mask) for i in range(ranks)])]
    psum x1 -> x0, blocking collectives: 38.9 us -> none  [on_device(): lax.psum(late_gains.astype(jnp.bfloat16), 'dp').astype(jnp.float32)]
  transfers between devices with their start and end apart: 11 -> 77, of which waited for: 11 -> 28; matrix products, arithmetic and copies ran while one was open for 10% -> 27% of each run, Pallas kernels for 0% -> 0%
where the time goes in v1:
time: 920 us; the launch traced here: 911 us
  waiting for transfers between devices  448 us (49%)
  matrix products  182 us (20%)
  local copies, waits for them, and re-layouts  136 us (15%)
  other arithmetic  64.5 us (7%)
  starting transfers between devices  63.2 us (7%)
  between operations  16.9 us (2%)
    ppermute x70, waiting for transfers between devices, flip(): return lax.ppermute(values, 'tensor', [(i, i ^ mask) for i in range(ranks)])  225 us
    psum x3, waiting for transfers between devices, total(): return lax.psum(jnp.concatenate(parts, axis=0), 'dp').astype(f32)  167 us
    all_to_all x4, waiting for transfers between devices, all_to_all(): lax.all_to_all(split_rows, 'dp', split_axis=0, concat_axis=0, tiled=True)  56 us
    dot_general x8, matrix products, matmul(): return jnp.dot(left_side, right_side, preferred_element_type=f32)  43 us
    dot_general x8, matrix products, matmul_tn(): lax.dot_general(left_side, right_side, (((0,), (0,)), ((), ())), preferre...  42 us
    ppermute x70, starting transfers between devices, flip(): return lax.ppermute(values, 'tensor', [(i, i ^ mask) for i in range(ranks)])  41.5 us
    dot_general x6, matrix products, matmul_nt(): lax.dot_general(left_side, right_side, (((1,), (1,)), ((), ())), preferre...  39.7 us
    squeeze x12, local copies, waits for them, and re-layouts, attention_forward(): queries, key_rows, value_rows = (rounded[0], rounded[1], rounded[2])  32.6 us
  transfers between devices with their start and end apart: 77, of which 28 were waited for; matrix products, arithmetic and copies ran while one was open for 27% of the time, Pallas kernels for 0%

profile of v1, /device:TPU:0, one launch (start us, length us, event | category | flops | bytes accessed | tf_op | source)
XLA Modules:
  0.0 910.7 jit_solution(1716265567482686442)
XLA Ops:
  36.7 6.0 collective-permute-done.4
  84.9 19.8 %collective-permute-done.10 = bf16[768,768]{1,0:T(8,128)(2,1)} collective-permute-done((bf16[768,768]{1,0:T(8,128)(2,1)}, bf16[768,768]{1,0:T(8,128)(2,1)}, u32[]{:S(2)}, u32[]{:S(2)}) %collective-permute-start.10) | collective-permute-done | bytes 1179680 | tf_op jit(solution)/shard_map/ppermute | solution.py:34
  117.6 9.3 %collective-permute-done.13 = bf16[3,192,768]{2,1,0:T(8,128)(2,1)S(1)} collective-permute-done((bf16[3,192,768]{2,1,0:T(8,128)(2,1)S(1)}, bf16[3,192,768]{2,1,0:T(8,128)(2,1)S(1)}, u32[]{:S(2)}, u32[]{:S(2)}) %collective-permute-start.13) | collective-permute-done | bytes 884768 | tf_op jit(solution)/shard_map/ppermute | solution.py:34
  173.1 13.2 %collective-permute-done.19 = bf16[400,768]{1,0:T(8,128)(2,1)} collective-permute-done((bf16[400,768]{1,0:T(8,128)(2,1)}, bf16[400,768]{1,0:T(8,128)(2,1)}, u32[]{:S(2)}, u32[]{:S(2)}) %collective-permute-start.19) | collective-permute-done | bytes 614432 | tf_op jit(solution)/shard_map/ppermute | solution.py:34
  188.7 5.5 fusion.44
  194.1 6.5 all-to-all-start
  200.6 14.8 %collective-permute-done.22 = bf16[768,768]{1,0:T(8,128)(2,1)} collective-permute-done((bf16[768,768]{1,0:T(8,128)(2,1)}, bf16[768,768]{1,0:T(8,128)(2,1)}, u32[]{:S(2)}, u32[]{:S(2)}) %collective-permute-start.22) | collective-permute-done | bytes 1179680 | tf_op jit(solution)/shard_map/ppermute | solution.py:34
  217.7 25.7 %collective-permute-done.25 = bf16[768,768]{1,0:T(8,128)(2,1)} collective-permute-done((bf16[768,768]{1,0:T(8,128)(2,1)}, bf16[768,768]{1,0:T(8,128)(2,1)}, u32[]{:S(2)}, u32[]{:S(2)}) %collective-permute-start.25) | collective-permute-done | bytes 1179680 | tf_op jit(solution)/shard_map/ppermute | solution.py:34
  243.4 6.8 fusion.74
  250.3 11.7 %convolution_convert_fusion.9 = bf16[832,768]{1,0:T(8,128)(2,1)} fusion(bf16[768,768]{1,0:T(8,128)(2,1)} %collective-permute-done.26, bf16[768,768]{1,0:T(8,128)(2,1)} %collective-permute-done.25, bf16[768,768]{1,0:T(8,128)(2,1)} %collective-permute-done.24, bf16[768,768]{1,0:T(8,128)(2,1)S(1)} %bitcast.229, f32[832,3072]{1,0:T(8,128)S(1)} %fusion.74), kind=kOutput, calls=%fused_computation.112 | convolution fusion | flops 3968385024 | bytes 16220160 | tf_op jit(solution)/shard_map/dot_general | solution.py:17
  262.0 6.4 all-to-all-start.1
  274.2 25.6 %all-to-all-done.1 = bf16[8,104,768]{2,1,0:T(8,128)(2,1)} async-done(((bf16[8,104,768]{2,1,0:T(8,128)(2,1)}), bf16[8,104,768]{2,1,0:T(8,128)(2,1)}, u32[]{:S(2)}, u32[]{:S(2)}) %all-to-all-start.1) | async-done | bytes 1277984 | tf_op jit(solution)/shard_map/all_to_all | solution.py:184
  320.3 19.9 %all-to-all-done.2 = bf16[8,104,768]{2,1,0:T(8,128)(2,1)} async-done(((bf16[8,104,768]{2,1,0:T(8,128)(2,1)}), bf16[8,104,768]{2,1,0:T(8,128)(2,1)}, u32[]{:S(2)}, u32[]{:S(2)}) %all-to-all-start.2) | async-done | bytes 1277984 | tf_op jit(solution)/shard_map/all_to_all | solution.py:184
  340.1 11.6 %convolution_convert_fusion = bf16[3072,768]{1,0:T(8,128)(2,1)} fusion(bf16[832,768]{1,0:T(8,128)(2,1)} %bitcast.30, f32[832,3072]{1,0:T(8,128)} %copy-done.86), kind=kOutput, calls=%fused_computation.20 | convolution fusion | flops 3951230976 | bytes 16220160 | tf_op jit(solution)/shard_map/dot_general | solution.py:21
  351.8 15.2 %fusion.6 = bf16[832,3072]{1,0:T(8,128)(2,1)S(1)} fusion(f32[832,3072]{1,0:T(8,128)} %copy-done.86, bf16[832,768]{1,0:T(8,128)(2,1)} %bitcast.30, bf16[768,768]{1,0:T(8,128)(2,1)} %collective-permute-done.26, bf16[768,768]{1,0:T(8,128)(2,1)} %collective-permute-done.25, bf16[768,768]{1,0:T(8,128)(2,1)} %collective-permute-done.24, ...), kind=kOutput, calls=%fused_computation.8 | convolution fusion | flops 3995860992 | bytes 21331968 | tf_op jit(solution)/shard_map/dot_general | solution.py:27
  367.0 9.0 convolution_convert_fusion.8
  380.4 7.6 convolution_convert_fusion.1
  400.1 10.6 %all-to-all-done.3 = bf16[8,104,768]{2,1,0:T(8,128)(2,1)} async-done(((bf16[8,104,768]{2,1,0:T(8,128)(2,1)}), bf16[8,104,768]{2,1,0:T(8,128)(2,1)}, u32[]{:S(2)}, u32[]{:S(2)}) %all-to-all-start.3) | async-done | bytes 1277984 | tf_op jit(solution)/shard_map/all_to_all | solution.py:184
  418.5 5.9 collective-permute-done.66
  430.2 19.4 %collective-permute-done.69 = bf16[768,768]{1,0:T(8,128)(2,1)} collective-permute-done((bf16[768,768]{1,0:T(8,128)(2,1)}, bf16[768,768]{1,0:T(8,128)(2,1)}, u32[]{:S(2)}, u32[]{:S(2)}) %collective-permute-start.69) | collective-permute-done | bytes 1179680 | tf_op jit(solution)/shard_map/ppermute | solution.py:34
  453.4 9.3 %collective-permute-done.35 = bf16[400,768]{1,0:T(8,128)(2,1)S(1)} collective-permute-done((bf16[400,768]{1,0:T(8,128)(2,1)S(1)}, bf16[400,768]{1,0:T(8,128)(2,1)S(1)}, u32[]{:S(2)}, u32[]{:S(2)}) %collective-permute-start.35) | collective-permute-done | bytes 614432 | tf_op jit(solution)/shard_map/ppermute | solution.py:34
  464.5 10.9 %collective-permute-done.29 = bf16[400,768]{1,0:T(8,128)(2,1)S(1)} collective-permute-done((bf16[400,768]{1,0:T(8,128)(2,1)S(1)}, bf16[400,768]{1,0:T(8,128)(2,1)S(1)}, u32[]{:S(2)}, u32[]{:S(2)}) %collective-permute-start.29) | collective-permute-done | bytes 614432 | tf_op jit(solution)/shard_map/ppermute | solution.py:34
  511.6 8.8 fusion.17
  568.6 5.5 convolution_convert_fusion.7
  591.2 6.0 collective-permute-done.53
  600.3 15.9 %collective-permute-done.50 = bf16[3,192,768]{2,1,0:T(8,128)(2,1)S(1)} collective-permute-done((bf16[3,192,768]{2,1,0:T(8,128)(2,1)S(1)}, bf16[3,192,768]{2,1,0:T(8,128)(2,1)S(1)}, u32[]{:S(2)}, u32[]{:S(2)}) %collective-permute-start.50) | collective-permute-done | bytes 884768 | tf_op jit(solution)/shard_map/ppermute | solution.py:34
  624.4 17.2 %collective-permute-done.58 = bf16[768,768]{1,0:T(8,128)(2,1)} collective-permute-done((bf16[768,768]{1,0:T(8,128)(2,1)}, bf16[768,768]{1,0:T(8,128)(2,1)}, u32[]{:S(2)}, u32[]{:S(2)}) %collective-permute-start.58) | collective-permute-done | bytes 1179680 | tf_op jit(solution)/shard_map/ppermute | solution.py:34
  644.6 22.3 %collective-permute-done.47 = bf16[768,768]{1,0:T(8,128)(2,1)} collective-permute-done((bf16[768,768]{1,0:T(8,128)(2,1)S(1)}, bf16[768,768]{1,0:T(8,128)(2,1)}, u32[]{:S(2)}, u32[]{:S(2)}) %collective-permute-start.47) | collective-permute-done | bytes 1179680 | tf_op jit(solution)/shard_map/ppermute | solution.py:34
  669.8 30.8 %all-reduce.11.cloned.1.call-done = bf16[778,768]{1,0:T(8,128)(2,1)} async-done(((bf16[778,768]{1,0:T(8,128)(2,1)}), bf16[778,768]{1,0:T(8,128)(2,1)}) %all-reduce.11.cloned.1.call-update) | async-done | bytes 1195024 | tf_op jit(solution)/shard_map/psum | solution.py:331
  724.4 13.6 %collective-permute-done.44 = bf16[3,192,768]{2,1,0:T(8,128)(2,1)S(1)} collective-permute-done((bf16[3,192,768]{2,1,0:T(8,128)(2,1)S(1)}, bf16[3,192,768]{2,1,0:T(8,128)(2,1)S(1)}, u32[]{:S(2)}, u32[]{:S(2)}) %collective-permute-start.44) | collective-permute-done | bytes 884768 | tf_op jit(solution)/shard_map/ppermute | solution.py:34
  739.5 74.3 %all-reduce.13.cloned.1.call-done = bf16[1536,768]{1,0:T(8,128)(2,1)} async-done(((bf16[1536,768]{1,0:T(8,128)(2,1)}), bf16[1536,768]{1,0:T(8,128)(2,1)}) %all-reduce.13.cloned.1.call-update) | async-done | bytes 2359312 | tf_op jit(solution)/shard_map/psum | solution.py:331
  835.5 62.3 %all-reduce.15.cloned.1.call-done = bf16[770,768]{1,0:T(8,128)(2,1)} async-done(((bf16[770,768]{1,0:T(8,128)(2,1)}), bf16[770,768]{1,0:T(8,128)(2,1)}) %all-reduce.15.cloned.1.call-update) | async-done | bytes 1182736 | tf_op jit(solution)/shard_map/psum | solution.py:331
  (587 shorter events, 366.3 us)
Async XLA Ops:
  13.1 35.0 %collective-permute-start = (bf16[3,192,768]{2,1,0:T(8,128)(2,1)}, bf16[3,192,768]{2,1,0:T(8,128)(2,1)}, u32[]{:S(2)}, u32[]{:S(2)}) collective-permute-start(bf16[3,192,768]{2,1,0:T(8,128)(2,1)} %get-tuple-element.87), channel_id=1, source_target_pairs={{0,1},{1,0},{2,3},{3,2},{4,5},{5,4},{6,7},{7,6},{8,9},{9,8},{10,11... | collective-permute-start | bytes 2654216 | tf_op jit(solution)/shard_map/ppermute | solution.py:34
  13.1 29.7 %collective-permute-start.9 = (bf16[768,768]{1,0:T(8,128)(2,1)}, bf16[768,768]{1,0:T(8,128)(2,1)}, u32[]{:S(2)}, u32[]{:S(2)}) collective-permute-start(bf16[768,768]{1,0:T(8,128)(2,1)} %param.20), channel_id=1, source_target_pairs={{0,1},{1,0},{2,3},{3,2},{4,5},{5,4},{6,7},{7,6},{8,9},{9,8},{10,11... | collective-permute-start | bytes 3538952 | tf_op jit(solution)/shard_map/ppermute | solution.py:34
  13.6 32.1 %collective-permute-start.6 = (bf16[768,768]{1,0:T(8,128)(2,1)}, bf16[768,768]{1,0:T(8,128)(2,1)}, u32[]{:S(2)}, u32[]{:S(2)}) collective-permute-start(bf16[768,768]{1,0:T(8,128)(2,1)} %param.19), channel_id=1, source_target_pairs={{0,1},{1,0},{2,3},{3,2},{4,5},{5,4},{6,7},{7,6},{8,9},{9,8},{10,11... | collective-permute-start | bytes 3538952 | tf_op jit(solution)/shard_map/ppermute | solution.py:34
  42.8 39.0 %collective-permute-start.3 = (bf16[192,768]{1,0:T(8,128)(2,1)}, bf16[192,768]{1,0:T(8,128)(2,1)}, u32[]{:S(2)}, u32[]{:S(2)}) collective-permute-start(bf16[192,768]{1,0:T(8,128)(2,1)} %get-tuple-element.20), channel_id=1, source_target_pairs={{0,1},{1,0},{2,3},{3,2},{4,5},{5,4},{6,7},{7,6},{8,9},{9,8},{10,11... | collective-permute-start | bytes 884744 | tf_op jit(solution)/shard_map/ppermute | solution.py:34
  42.8 93.4 %collective-permute-start.12 = (bf16[3,192,768]{2,1,0:T(8,128)(2,1)}, bf16[3,192,768]{2,1,0:T(8,128)(2,1)}, u32[]{:S(2)}, u32[]{:S(2)}) collective-permute-start(bf16[3,192,768]{2,1,0:T(8,128)(2,1)} %get-tuple-element.23), channel_id=1, source_target_pairs={{0,1},{1,0},{2,3},{3,2},{4,5},{5,4},{6,7},{7,6},{8,9},{9,8},{10,11... | collective-permute-start | bytes 2654216 | tf_op jit(solution)/shard_map/ppermute | solution.py:34
  45.6 119.3 %collective-permute-start.15 = (bf16[192,768]{1,0:T(8,128)(2,1)}, bf16[192,768]{1,0:T(8,128)(2,1)}, u32[]{:S(2)}, u32[]{:S(2)}) collective-permute-start(bf16[192,768]{1,0:T(8,128)(2,1)} %get-tuple-element.24), channel_id=1, source_target_pairs={{0,1},{1,0},{2,3},{3,2},{4,5},{5,4},{6,7},{7,6},{8,9},{9,8},{10,11... | collective-permute-start | bytes 884744 | tf_op jit(solution)/shard_map/ppermute | solution.py:34
  49.9 31.9 %collective-permute-start.5 = (bf16[192,768]{1,0:T(8,128)(2,1)}, bf16[192,768]{1,0:T(8,128)(2,1)}, u32[]{:S(2)}, u32[]{:S(2)}) collective-permute-start(bf16[192,768]{1,0:T(8,128)(2,1)} %collective-permute-done.4), channel_id=1, source_target_pairs={{0,1},{1,0},{2,3},{3,2},{4,5},{5,4},{6,7},{7,6},{8,9},{9,8},{10,11... | collective-permute-start | bytes 884744 | tf_op jit(solution)/shard_map/ppermute | solution.py:34
  194.1 49.2 %all-to-all-start = ((bf16[8,104,768]{2,1,0:T(8,128)(2,1)}), bf16[8,104,768]{2,1,0:T(8,128)(2,1)}, u32[]{:S(2)}, u32[]{:S(2)}) async-start(bf16[8,104,768]{2,1,0:T(8,128)(2,1)} %bitcast.212), calls=%async_computation | async-start | bytes 2555904 | tf_op jit(solution)/shard_map/all_to_all | solution.py:184
  217.7 32.6 %collective-permute-start.24 = (bf16[768,768]{1,0:T(8,128)(2,1)}, bf16[768,768]{1,0:T(8,128)(2,1)}, u32[]{:S(2)}, u32[]{:S(2)}) collective-permute-start(bf16[768,768]{1,0:T(8,128)(2,1)} %bitcast.228), channel_id=1, source_target_pairs={{0,1},{1,0},{2,3},{3,2},{4,5},{5,4},{6,7},{7,6},{8,9},{9,8},{10,11... | collective-permute-start | bytes 3538952 | tf_op jit(solution)/shard_map/ppermute | solution.py:34
  262.0 37.8 %all-to-all-start.1 = ((bf16[8,104,768]{2,1,0:T(8,128)(2,1)}), bf16[8,104,768]{2,1,0:T(8,128)(2,1)}, u32[]{:S(2)}, u32[]{:S(2)}) async-start(bf16[8,104,768]{2,1,0:T(8,128)(2,1)} %bitcast.211), calls=%async_computation.1 | async-start | bytes 2555904 | tf_op jit(solution)/shard_map/all_to_all | solution.py:184
  305.1 35.0 %all-to-all-start.2 = ((bf16[8,104,768]{2,1,0:T(8,128)(2,1)}), bf16[8,104,768]{2,1,0:T(8,128)(2,1)}, u32[]{:S(2)}, u32[]{:S(2)}) async-start(bf16[8,104,768]{2,1,0:T(8,128)(2,1)} %bitcast.210), calls=%async_computation.2 | async-start | bytes 2555904 | tf_op jit(solution)/shard_map/all_to_all | solution.py:184
  311.7 81.6 %collective-permute-start.36 = (f32[832]{0:T(1024)S(1)}, f32[832]{0:T(1024)S(1)}, u32[]{:S(2)}, u32[]{:S(2)}) collective-permute-start(f32[832]{0:T(1024)S(1)} %get-tuple-element.64), channel_id=1, source_target_pairs={{0,1},{1,0},{2,3},{3,2},{4,5},{5,4},{6,7},{7,6},{8,9},{9,8},{10,11... | collective-permute-start | bytes 9992 | tf_op jit(solution)/shard_map/ppermute | solution.py:34
  319.6 96.0 %collective-permute-start.28 = (bf16[400,768]{1,0:T(8,128)(2,1)}, bf16[400,768]{1,0:T(8,128)(2,1)S(1)}, u32[]{:S(2)}, u32[]{:S(2)}) collective-permute-start(bf16[400,768]{1,0:T(8,128)(2,1)} %get-tuple-element.77), channel_id=1, source_target_pairs={{0,1},{1,0},{2,3},{3,2},{4,5},{5,4},{6,7},{7,6},{8,9},{9,8},{10,11... | collective-permute-start | bytes 1843208 | tf_op jit(solution)/shard_map/ppermute | solution.py:34
  320.2 73.6 %collective-permute-start.38 = (f32[832]{0:T(1024)S(1)}, f32[832]{0:T(1024)S(1)}, u32[]{:S(2)}, u32[]{:S(2)}) collective-permute-start(f32[832]{0:T(1024)S(1)} %collective-permute-done.37), channel_id=1, source_target_pairs={{0,1},{1,0},{2,3},{3,2},{4,5},{5,4},{6,7},{7,6},{8,9},{9,8},{10,11... | collective-permute-start | bytes 9992 | tf_op jit(solution)/shard_map/ppermute | solution.py:34
  376.0 34.6 %all-to-all-start.3 = ((bf16[8,104,768]{2,1,0:T(8,128)(2,1)}), bf16[8,104,768]{2,1,0:T(8,128)(2,1)}, u32[]{:S(2)}, u32[]{:S(2)}) async-start(bf16[8,104,768]{2,1,0:T(8,128)(2,1)} %bitcast.209), calls=%async_computation.3 | async-start | bytes 2555904 | tf_op jit(solution)/shard_map/all_to_all | solution.py:184
  380.3 320.3 %all-reduce.11.cloned.1.call-start = ((), (), s32[]{:S(2)}) async-start(), calls=%async_computation.4 | async-start | bytes 2408448 | tf_op jit(solution)/shard_map/psum | solution.py:331
  394.9 34.8 %collective-permute-start.67 = (bf16[768,768]{1,0:T(8,128)(2,1)}, bf16[768,768]{1,0:T(8,128)(2,1)}, u32[]{:S(2)}, u32[]{:S(2)}) collective-permute-start(bf16[768,768]{1,0:T(8,128)(2,1)} %get-tuple-element.52), channel_id=1, source_target_pairs={{0,1},{1,0},{2,3},{3,2},{4,5},{5,4},{6,7},{7,6},{8,9},{9,8},{10,11... | collective-permute-start | bytes 3538952 | tf_op jit(solution)/shard_map/ppermute | solution.py:34
  399.6 50.0 %collective-permute-start.69 = (bf16[768,768]{1,0:T(8,128)(2,1)}, bf16[768,768]{1,0:T(8,128)(2,1)}, u32[]{:S(2)}, u32[]{:S(2)}) collective-permute-start(bf16[768,768]{1,0:T(8,128)(2,1)} %add_convert_fusion.1), channel_id=1, source_target_pairs={{0,2},{1,3},{2,0},{3,1},{4,6},{5,7},{6,4},{7,5},{8,10},{9,11},{10,... | collective-permute-start | bytes 3538952 | tf_op jit(solution)/shard_map/ppermute | solution.py:34
  417.7 46.8 %collective-permute-start.27 = (bf16[400,768]{1,0:T(8,128)(2,1)S(1)}, bf16[400,768]{1,0:T(8,128)(2,1)S(1)}, u32[]{:S(2)}, u32[]{:S(2)}) collective-permute-start(bf16[400,768]{1,0:T(8,128)(2,1)S(1)} %copy-done.51), channel_id=1, source_target_pairs={{0,1},{1,0},{2,3},{3,2},{4,5},{5,4},{6,7},{7,6},{8,9},{9,8},{10,11... | collective-permute-start | bytes 1843208 | tf_op jit(solution)/shard_map/ppermute | solution.py:34
  418.1 35.4 %collective-permute-start.33 = (bf16[400,768]{1,0:T(8,128)(2,1)S(1)}, bf16[400,768]{1,0:T(8,128)(2,1)S(1)}, u32[]{:S(2)}, u32[]{:S(2)}) collective-permute-start(bf16[400,768]{1,0:T(8,128)(2,1)S(1)} %get-tuple-element.70), channel_id=1, source_target_pairs={{0,1},{1,0},{2,3},{3,2},{4,5},{5,4},{6,7},{7,6},{8,9},{9,8},{10,11... | collective-permute-start | bytes 1843208 | tf_op jit(solution)/shard_map/ppermute | solution.py:34
  424.4 38.3 %collective-permute-start.35 = (bf16[400,768]{1,0:T(8,128)(2,1)S(1)}, bf16[400,768]{1,0:T(8,128)(2,1)S(1)}, u32[]{:S(2)}, u32[]{:S(2)}) collective-permute-start(bf16[400,768]{1,0:T(8,128)(2,1)S(1)} %add_convert_fusion.20), channel_id=1, source_target_pairs={{0,2},{1,3},{2,0},{3,1},{4,6},{5,7},{6,4},{7,5},{8,10},{9,11},{10,... | collective-permute-start | bytes 1843208 | tf_op jit(solution)/shard_map/ppermute | solution.py:34
  429.7 45.7 %collective-permute-start.29 = (bf16[400,768]{1,0:T(8,128)(2,1)S(1)}, bf16[400,768]{1,0:T(8,128)(2,1)S(1)}, u32[]{:S(2)}, u32[]{:S(2)}) collective-permute-start(bf16[400,768]{1,0:T(8,128)(2,1)S(1)} %add_convert_fusion.24), channel_id=1, source_target_pairs={{0,2},{1,3},{2,0},{3,1},{4,6},{5,7},{6,4},{7,5},{8,10},{9,11},{10,... | collective-permute-start | bytes 1843208 | tf_op jit(solution)/shard_map/ppermute | solution.py:34
  599.3 44.7 %collective-permute-start.45 = (bf16[768,768]{1,0:T(8,128)(2,1)}, bf16[768,768]{1,0:T(8,128)(2,1)}, u32[]{:S(2)}, u32[]{:S(2)}) collective-permute-start(bf16[768,768]{1,0:T(8,128)(2,1)} %get-tuple-element.56), channel_id=1, source_target_pairs={{0,1},{1,0},{2,3},{3,2},{4,5},{5,4},{6,7},{7,6},{8,9},{9,8},{10,11... | collective-permute-start | bytes 3538952 | tf_op jit(solution)/shard_map/ppermute | solution.py:34
  599.7 41.9 %collective-permute-start.58 = (bf16[768,768]{1,0:T(8,128)(2,1)}, bf16[768,768]{1,0:T(8,128)(2,1)}, u32[]{:S(2)}, u32[]{:S(2)}) collective-permute-start(bf16[768,768]{1,0:T(8,128)(2,1)} %add_convert_fusion.7), channel_id=1, source_target_pairs={{0,2},{1,3},{2,0},{3,1},{4,6},{5,7},{6,4},{7,5},{8,10},{9,11},{10,... | collective-permute-start | bytes 3538952 | tf_op jit(solution)/shard_map/ppermute | solution.py:34
  616.2 50.7 %collective-permute-start.47 = (bf16[768,768]{1,0:T(8,128)(2,1)S(1)}, bf16[768,768]{1,0:T(8,128)(2,1)}, u32[]{:S(2)}, u32[]{:S(2)}) collective-permute-start(bf16[768,768]{1,0:T(8,128)(2,1)S(1)} %add_convert_fusion.10), channel_id=1, source_target_pairs={{0,2},{1,3},{2,0},{3,1},{4,6},{5,7},{6,4},{7,5},{8,10},{9,11},{10,... | collective-permute-start | bytes 3538952 | tf_op jit(solution)/shard_map/ppermute | solution.py:34
  618.2 195.6 %all-reduce.13.cloned.1.call-start = ((), (), s32[]{:S(2)}) async-start(), calls=%async_computation.5 | async-start | bytes 4718592 | tf_op jit(solution)/shard_map/psum | solution.py:331
  621.2 92.4 %collective-permute-start.31 = (bf16[400,768]{1,0:T(8,128)(2,1)S(1)}, bf16[400,768]{1,0:T(8,128)(2,1)}, u32[]{:S(2)}, u32[]{:S(2)}) collective-permute-start(bf16[400,768]{1,0:T(8,128)(2,1)S(1)} %copy-done.41), channel_id=1, source_target_pairs={{0,2},{1,3},{2,0},{3,1},{4,6},{5,7},{6,4},{7,5},{8,10},{9,11},{10,... | collective-permute-start | bytes 1843208 | tf_op jit(solution)/shard_map/ppermute | solution.py:34
  623.8 82.8 %collective-permute-start.40 = (bf16[400,768]{1,0:T(8,128)(2,1)}, bf16[400,768]{1,0:T(8,128)(2,1)}, u32[]{:S(2)}, u32[]{:S(2)}) collective-permute-start(bf16[400,768]{1,0:T(8,128)(2,1)} %add_convert_fusion.18), channel_id=1, source_target_pairs={{0,2},{1,3},{2,0},{3,1},{4,6},{5,7},{6,4},{7,5},{8,10},{9,11},{10,... | collective-permute-start | bytes 1843208 | tf_op jit(solution)/shard_map/ppermute | solution.py:34
  641.6 65.0 %collective-permute-start.59 = (bf16[192,768]{1,0:T(8,128)(2,1)}, bf16[192,768]{1,0:T(8,128)(2,1)}, u32[]{:S(2)}, u32[]{:S(2)}) collective-permute-start(bf16[192,768]{1,0:T(8,128)(2,1)} %get-tuple-element.90), channel_id=1, source_target_pairs={{0,1},{1,0},{2,3},{3,2},{4,5},{5,4},{6,7},{7,6},{8,9},{9,8},{10,11... | collective-permute-start | bytes 884744 | tf_op jit(solution)/shard_map/ppermute | solution.py:34
  644.0 70.1 %collective-permute-start.43 = (bf16[3,192,768]{2,1,0:T(8,128)(2,1)}, bf16[3,192,768]{2,1,0:T(8,128)(2,1)}, u32[]{:S(2)}, u32[]{:S(2)}) collective-permute-start(bf16[3,192,768]{2,1,0:T(8,128)(2,1)} %get-tuple-element.61), channel_id=1, source_target_pairs={{0,1},{1,0},{2,3},{3,2},{4,5},{5,4},{6,7},{7,6},{8,9},{9,8},{10,11... | collective-permute-start | bytes 2654216 | tf_op jit(solution)/shard_map/ppermute | solution.py:34
  666.9 36.6 %collective-permute-start.63 = (bf16[2,768]{1,0:T(2,128)(2,1)S(1)}, bf16[2,768]{1,0:T(2,128)(2,1)S(1)}, u32[]{:S(2)}, u32[]{:S(2)}) collective-permute-start(bf16[2,768]{1,0:T(2,128)(2,1)S(1)} %add_convert_fusion.35), channel_id=1, source_target_pairs={{0,2},{1,3},{2,0},{3,1},{4,6},{5,7},{6,4},{7,5},{8,10},{9,11},{10,... | collective-permute-start | bytes 9224 | tf_op jit(solution)/shard_map/ppermute | solution.py:34
  706.5 191.2 %all-reduce.15.cloned.1.call-start = ((), (), s32[]{:S(2)}) async-start(), calls=%async_computation.6 | async-start | bytes 2383872 | tf_op jit(solution)/shard_map/psum | solution.py:331
  (146 other events, 1904.1 us)
Sparse Core Ops, SparseCore 0:
  618.3 82.1 all-reduce.10
  706.6 107.1 all-reduce.12
  817.8 79.9 all-reduce.14

commit v2 on v1

--- a/solution.py
+++ b/solution.py
@@ -1,11 +1,13 @@
 import jax
 import jax.numpy as jnp
 from jax import lax
+from jax.experimental import pallas as pl
+from jax.experimental.pallas import tpu as pltpu
 from jax.sharding import PartitionSpec as P
 
 HD = 64
 SEQ = 197
-PAD = 200
+PAD = 208
 
 epsilon = 1e-06
 highest = lax.Precision.HIGHEST
@@ -56,10 +58,61 @@
     return (left_side.astype(f32) + right_side.astype(f32)).astype(bf16)
 
 
-def scatter_sum(parts):
+def near_sum(parts):
     mine = add_rounded(parts[0], flip(parts[1], 1))
     other = add_rounded(parts[2], flip(parts[3], 1))
-    return add_rounded(mine, flip(other, 2))
+    return (mine, other)
+
+
+def far_sum(pair, earlier=None):
+    mine, other = pair
+    return add_rounded(mine, far(other, earlier))
+
+
+def dp_flip(values, bit):
+    groups = lax.axis_size("dp")
+    return lax.ppermute(values, "dp", [(i, i ^ (1 << bit)) for i in range(groups)])
+
+
+def dp_bits():
+    return list(range(lax.axis_size("dp").bit_length() - 1))
+
+
+def upper(bit):
+    return (lax.axis_index("dp") >> bit) % 2 == 1
+
+
+def dp_halve(values, bit):
+    half = values.shape[0] // 2
+    low, high = values[:half], values[half:]
+    kept = jnp.where(upper(bit), high, low)
+    sent = jnp.where(upper(bit), low, high)
+    return add_rounded(kept, dp_flip(sent, bit))
+
+
+def dp_double(values, bit):
+    arrived = dp_flip(values, bit)
+    return jnp.concatenate(
+        [jnp.where(upper(bit), arrived, values), jnp.where(upper(bit), values, arrived)], axis=0
+    )
+
+
+def dp_halves(values, bits):
+    for bit in bits:
+        values = dp_halve(values, bit)
+    return values
+
+
+def dp_doubles(values, bits):
+    for bit in reversed(bits):
+        values = dp_double(values, bit)
+    return values
+
+
+def dp_rows(*parts):
+    rows = jnp.concatenate(parts, axis=0)
+    unit = 8 * lax.axis_size("dp")
+    return jnp.pad(rows, ((0, -rows.shape[0] % unit), (0, 0)))
 
 
 def norm_forward(values, norm_gain):
@@ -79,60 +132,110 @@
     return (grad_in, jnp.sum(grad_out * unit_rows, axis=0))
 
 
-def masked_scores(queries, key_rows):
-    scores = jnp.einsum(
-        "ishd,ithd->ihst", queries, key_rows, preferred_element_type=f32
-    ) * HD ** (-0.5)
-    return jnp.where(jnp.arange(PAD) < SEQ, scores, -1e30)
+def half_masks():
+    lane = lax.broadcasted_iota(jnp.int32, (1, 2 * HD), 1)
+    return [(lane // HD == one).astype(f32).astype(bf16) for one in range(2)]
+
+
+def head_probs(queries, key_rows):
+    scores = matmul_nt(queries, key_rows) * HD ** (-0.5)
+    column = lax.broadcasted_iota(jnp.int32, (1, PAD), 1)
+    scores = jnp.where(column < SEQ, scores, -1e30)
+    weights = jnp.exp(scores - jnp.max(scores, axis=-1, keepdims=True))
+    return weights / jnp.sum(weights, axis=-1, keepdims=True)
+
+
+def context_kernel(qkv_ref, context_ref):
+    masks = half_masks()
+    for first in range(0, context_ref.shape[1], 2 * HD):
+        columns = slice(first, first + 2 * HD)
+        queries, key_rows, value_rows = (qkv_ref[one, 0, :, columns] for one in range(3))
+        total = 0.0
+        for mask in masks:
+            weights = head_probs(queries * mask, key_rows).astype(bf16)
+            total = total + matmul(weights, value_rows * mask)
+        context_ref[:, columns] = total.astype(bf16)
+
+
+def context_grad_kernel(qkv_ref, grad_ref, out_ref):
+    masks = half_masks()
+    scale = HD ** (-0.5)
+    for first in range(0, grad_ref.shape[1], 2 * HD):
+        columns = slice(first, first + 2 * HD)
+        queries, key_rows, value_rows = (qkv_ref[one, 0, :, columns] for one in range(3))
+        grad_context = grad_ref[:, columns]
+        grad_queries, grad_keys, grad_values = 0.0, 0.0, 0.0
+        for mask in masks:
+            own_queries, own_grad = queries * mask, grad_context * mask
+            probs = head_probs(own_queries, key_rows)
+            grad_weights = matmul_nt(own_grad, value_rows)
+            grad_values = grad_values + matmul_tn(probs.astype(bf16), own_grad)
+            grad_scores = probs * (
+                grad_weights - jnp.sum(probs * grad_weights, axis=-1, keepdims=True)
+            )
+            grad_scores = grad_scores.astype(bf16)
+            grad_queries = grad_queries + matmul(grad_scores, key_rows * mask)
+            grad_keys = grad_keys + matmul_tn(grad_scores, own_queries)
+        out_ref[0, 0, :, columns] = (grad_queries * scale).astype(bf16)
+        out_ref[1, 0, :, columns] = (grad_keys * scale).astype(bf16)
+        out_ref[2, 0, :, columns] = grad_values.astype(bf16)
+
+
+def attend(qkv):
+    images, width = qkv.shape[1], qkv.shape[3]
+    return pl.pallas_call(
+        context_kernel,
+        grid=(images,),
+        in_specs=[pl.BlockSpec((3, 1, PAD, width), lambda i: (0, i, 0, 0))],
+        out_specs=pl.BlockSpec((PAD, width), lambda i: (i, 0)),
+        out_shape=jax.ShapeDtypeStruct((images * PAD, width), bf16),
+        compiler_params=pltpu.CompilerParams(vmem_limit_bytes=32 * 1024 * 1024),
+        cost_estimate=pl.CostEstimate(
+            flops=4 * images * PAD * PAD * width,
+            bytes_accessed=8 * images * PAD * width,
+            transcendentals=images * PAD * PAD * width // HD,
+        ),
+    )(qkv)
+
+
+def attend_grad(qkv, grad_context):
+    images, width = qkv.shape[1], qkv.shape[3]
+    return pl.pallas_call(
+        context_grad_kernel,
+        grid=(images,),
+        in_specs=[
+            pl.BlockSpec((3, 1, PAD, width), lambda i: (0, i, 0, 0)),
+            pl.BlockSpec((PAD, width), lambda i: (i, 0)),
+        ],
+        out_specs=pl.BlockSpec((3, 1, PAD, width), lambda i: (0, i, 0, 0)),
+        out_shape=jax.ShapeDtypeStruct(qkv.shape, bf16),
+        compiler_params=pltpu.CompilerParams(vmem_limit_bytes=32 * 1024 * 1024),
+        cost_estimate=pl.CostEstimate(
+            flops=10 * images * PAD * PAD * width,
+            bytes_accessed=14 * images * PAD * width,
+            transcendentals=images * PAD * PAD * width // HD,
+        ),
+    )(qkv, grad_context)
 
 
 def attention_forward(stream, norm_gain, qkv_w, proj_w):
     normed, unit_rows, inverse = norm_forward(stream, norm_gain)
     normed_b = normed.astype(bf16)
-    tokens = normed_b.shape[0]
     projected = jnp.einsum("td,jcd->jtc", normed_b, qkv_w, preferred_element_type=f32)
-    rounded = projected.astype(bf16).reshape(3, tokens // PAD, PAD, -1, HD)
-    queries, key_rows, value_rows = (rounded[0], rounded[1], rounded[2])
-    scores = masked_scores(queries, key_rows)
-    row_peak = jnp.max(scores, axis=-1, keepdims=True)
-    weights = jnp.exp(scores - row_peak)
-    row_total = jnp.sum(weights, axis=-1, keepdims=True)
-    log_total = row_peak + jnp.log(row_total)
-    weights_b = (weights / row_total).astype(bf16)
-    context = jnp.einsum("ihst,ithd->ishd", weights_b, value_rows, preferred_element_type=f32)
-    context = context.astype(bf16).reshape(tokens, -1)
-    return (
-        stream + matmul(context, proj_w),
-        (unit_rows, inverse, normed_b, queries, key_rows, value_rows, log_total, context),
-    )
-
-
-def attention_backward(grad_stream, norm_gain, qkv_w, proj_w, saved_state):
-    unit_rows, inverse, normed_b, queries, key_rows, value_rows, log_total, context = saved_state
+    qkv = projected.astype(bf16).reshape(3, -1, PAD, qkv_w.shape[1])
+    context = attend(qkv)
+    return (stream + matmul(context, proj_w), (unit_rows, inverse, normed_b, qkv, context))
+
+
+def attention_backward(grad_stream, norm_gain, qkv_w, proj_w, saved_state, between=None):
+    unit_rows, inverse, normed_b, qkv, context = saved_state
     tokens = normed_b.shape[0]
     grad_branch = grad_stream.astype(bf16)
     grad_proj = matmul_tn(context, grad_branch)
-    grad_context = matmul_nt(grad_branch, proj_w).astype(bf16).reshape(queries.shape)
-    probs_again = jnp.exp(masked_scores(queries, key_rows) - log_total)
-    grad_weights = jnp.einsum(
-        "ishd,ithd->ihst", grad_context, value_rows, preferred_element_type=f32
-    )
-    grad_values = jnp.einsum(
-        "ihst,ishd->ithd", probs_again.astype(bf16), grad_context, preferred_element_type=f32
-    )
-    grad_scores = probs_again * (
-        grad_weights - jnp.sum(probs_again * grad_weights, axis=-1, keepdims=True)
-    )
-    grad_scores = grad_scores.astype(bf16)
-    grad_queries = jnp.einsum(
-        "ihst,ithd->ishd", grad_scores, key_rows, preferred_element_type=f32
-    ) * HD ** (-0.5)
-    grad_keys = jnp.einsum(
-        "ihst,ishd->ithd", grad_scores, queries, preferred_element_type=f32
-    ) * HD ** (-0.5)
-    stacked = (
-        jnp.stack([grad_queries, grad_keys, grad_values]).astype(bf16).reshape(3, tokens, -1)
-    )
+    grad_context = matmul_nt(grad_branch, proj_w).astype(bf16)
+    stacked = attend_grad(qkv, grad_context).reshape(3, tokens, -1)
+    if between is not None:
+        stacked = between(stacked)
     grad_qkv = jnp.einsum("jtc,td->jcd", stacked, normed_b, preferred_element_type=f32)
     grad_normed = jnp.einsum("jtc,jcd->td", stacked, qkv_w, preferred_element_type=f32)
     grad_in, grad_gain = norm_backward(grad_normed, norm_gain, unit_rows, inverse)
@@ -227,6 +330,7 @@
     far_down = far(dense_down, far_up)
     far_qkv1 = far(qkv_t[1], far_down)
     far_proj1 = far(attn_proj[1], far_qkv1)
+    far_ex_up = far(expert_up[0], far_proj1)
     qkv0 = jnp.concatenate(near(qkv_t[0], far_qkv0), axis=1)
     proj0 = jnp.concatenate(near(attn_proj[0], far_proj0), axis=0)
     up_w = jnp.concatenate(near(dense_up, far_up), axis=1)
@@ -265,10 +369,9 @@
 
     normed, unit_rows, inverse = norm_forward(stream3, norm_gains[1, 1])
     normed_b = normed.astype(bf16)
-    far_normed = far(normed_b, far_proj1)
+    far_normed = far(normed_b)
     normed_all = jnp.concatenate(near(normed_b, far_normed), axis=0)
-    far_ex_up = far(expert_up[0], far_normed)
-    far_ex_down = far(expert_down[0], far_ex_up)
+    far_ex_down = far(expert_down[0], (far_normed, far_ex_up))
     ex_up = jnp.concatenate(near(expert_up[0], far_ex_up), axis=1)
     ex_down = jnp.concatenate(near(expert_down[0], far_ex_down), axis=0)
 
@@ -292,14 +395,14 @@
     unused_out, gelu_back = jax.vjp(jax.nn.gelu, hidden_pre)
     grad_pre = gelu_back(matmul_nt(grad_rows, ex_down))[0].astype(bf16)
     grad_back = all_to_all(matmul_nt(grad_pre, ex_up).astype(bf16))
-    grad_ex_down = scatter_sum(row_parts(matmul_tn(hidden_b, grad_rows).astype(bf16), 0))
-    grad_ex_up = scatter_sum(row_parts(matmul_tn(rows_in, grad_pre).astype(bf16), 1))
+    down_pair = near_sum(row_parts(matmul_tn(hidden_b, grad_rows).astype(bf16), 0))
+    grad_ex_down = far_sum(down_pair)
+    up_pair = near_sum(row_parts(matmul_tn(rows_in, grad_pre).astype(bf16), 1))
+    grad_back, up_pair, grad_ex_down = lax.optimization_barrier((grad_back, up_pair, grad_ex_down))
 
     out_f = rows_out.astype(f32)
     gate_grad_slot = jnp.sum(cot_slot * out_f, axis=1)
     branch = matmul_tn(pick, (gate_slot * out_f).astype(bf16)).astype(bf16)
-    stream4 = stream3 + scatter_sum(row_parts(branch, 0)).astype(f32)
-    block_output = in_order(gather(stream4.astype(bf16)), me)
 
     own_holder = blocked(holder)[:, 0]
     own_place = blocked(place)[:, 0]
@@ -317,8 +420,9 @@
     )
     grad_router = jnp.dot(normed_b.astype(f32).T, grad_logits, precision=highest)
     grad_branch = matmul_tn(pick, grad_back).astype(bf16)
-    grad_normed = scatter_sum(row_parts(grad_branch, 0)).astype(f32)
-    grad_normed = grad_normed + jnp.dot(grad_logits, router_weight.T, precision=highest)
+    grad_normed = far_sum(near_sum(row_parts(grad_branch, 0)))
+    grad_ex_up = far_sum(up_pair, grad_normed)
+    grad_normed = grad_normed.astype(f32) + jnp.dot(grad_logits, router_weight.T, precision=highest)
     grad_in, gain_expert = norm_backward(grad_normed, norm_gains[1, 1], unit_rows, inverse)
     grad3 = grad_out + grad_in
 
@@ -327,51 +431,82 @@
         values = add_rounded(values, flip(values, 1))
         return add_rounded(values, flip(values, 2))
 
-    def total(*parts):
-        return lax.psum(jnp.concatenate(parts, axis=0), "dp").astype(f32)
-
-    def qkv_rows(grad_qkv):
-        own = scatter_sum(row_parts(grad_qkv, 1))
-        return own.reshape(-1, width)
+    columns = attn_qkv.shape[3]
+    bits = dp_bits()
+
+    def attn_pair(grad_qkv, grad_proj):
+        pairs = [near_sum(row_parts(grad_qkv, 1)), near_sum(row_parts(grad_proj, 0))]
+        return tuple(
+            jnp.concatenate([qkv_part.reshape(-1, width), proj_part], axis=0)
+            for qkv_part, proj_part in zip(*pairs)
+        )
 
     grad2, grad_qkv1, grad_proj1, gain_attn1 = attention_backward(
         grad3, norm_gains[1, 0], qkv1, proj1, attn1_state
     )
+    attn1_pair = attn_pair(grad_qkv1, grad_proj1)
     smalls1 = small_sum(
         jnp.concatenate([gain_attn1[None], gain_expert[None], grad_router.T], axis=0)
     )
-    sums1 = total(qkv_rows(grad_qkv1), scatter_sum(row_parts(grad_proj1, 0)), smalls1)
+    grad2, attn1_pair, grad_ex_up = lax.optimization_barrier((grad2, attn1_pair, grad_ex_up))
+    attn1_sum = far_sum(attn1_pair)
     grad1, grad_up, grad_down, gain_dense = dense_backward(
         grad2, norm_gains[0, 1], up_w, down_w, dense_state
     )
-    down_part = scatter_sum(row_parts(grad_down, 0))
-    up_part = scatter_sum(row_parts(grad_up, 1))
-    sums_dense = total(after(up_part, sums1), down_part)
+    down_pair = near_sum(row_parts(grad_down, 0))
+    up_pair = near_sum(row_parts(grad_up, 1))
+    grad1, down_pair, up_pair, attn1_sum, smalls1 = lax.optimization_barrier(
+        (grad1, down_pair, up_pair, attn1_sum, smalls1)
+    )
+    attn1_part = dp_halve(dp_rows(attn1_sum, smalls1), bits[0])
+    down_sum = far_sum(down_pair)
+
+    def between(values):
+        nonlocal attn1_part, down_sum
+        values, attn1_part, down_sum = lax.optimization_barrier((values, attn1_part, down_sum))
+        return values
+
     grad0, grad_qkv0, grad_proj0, gain_attn0 = attention_backward(
-        grad1, norm_gains[0, 0], qkv0, proj0, attn0_state
-    )
+        grad1, norm_gains[0, 0], qkv0, proj0, attn0_state, between
+    )
+    attn1_part = dp_halves(attn1_part, bits[1:])
+    down_part = dp_halve(dp_rows(down_sum), bits[0])
+    attn0_pair = attn_pair(grad_qkv0, grad_proj0)
     smalls0 = small_sum(jnp.concatenate([gain_attn0[None], gain_dense[None]], axis=0))
-    proj_part0 = scatter_sum(row_parts(grad_proj0, 0))
-    sums0 = total(after(qkv_rows(grad_qkv0), sums_dense), proj_part0, smalls0)
-    input_grad = in_order(gather(grad0.astype(bf16)), me).astype(f32)
-
-    columns = attn_qkv.shape[3]
+    up_sum = far_sum(up_pair, down_sum)
+    attn0_sum = far_sum(attn0_pair, up_sum)
+    down_part = dp_halves(down_part, bits[1:])
+    up_part = dp_halves(dp_rows(up_sum), bits)
+    attn0_part = dp_halves(dp_rows(attn0_sum, smalls0), bits)
+    sums1 = dp_doubles(attn1_part, bits).astype(f32)
+    sums_down = dp_doubles(down_part, bits).astype(f32)
+    sums_up = dp_doubles(up_part, bits).astype(f32)
+    sums0 = dp_doubles(attn0_part, bits).astype(f32)
+
+    grad0_b = grad0.astype(bf16)
+    far_grad0 = far(grad0_b, attn0_sum)
+    input_grad = in_order(near(grad0_b, far_grad0), me).astype(f32)
+    branch_sum = far_sum(near_sum(row_parts(branch, 0)), far_grad0)
+    stream4 = (stream3 + branch_sum.astype(f32)).astype(bf16)
+    block_output = in_order(near(stream4, far(stream4)), me)
+
     grad_qkv = jnp.stack(
-        [jnp.swapaxes(sums[: 3 * columns].reshape(3, columns, width), 1, 2) for sums in (sums0, sums1)]
+        [
+            jnp.swapaxes(sums[: 3 * columns].reshape(3, columns, width), 1, 2)
+            for sums in (sums0, sums1)
+        ]
     )
     grad_proj = jnp.stack([sums[3 * columns : 4 * columns] for sums in (sums0, sums1)])
-    grad_gains = jnp.stack(
-        [sums[4 * columns : 4 * columns + 2] for sums in (sums0, sums1)]
-    )
-    router_grad = sums1[4 * columns + 2 :].T
+    grad_gains = jnp.stack([sums[4 * columns : 4 * columns + 2] for sums in (sums0, sums1)])
+    router_grad = sums1[4 * columns + 2 : 4 * columns + 2 + experts].T
     return (
         block_output,
         input_grad,
         grad_gains,
         grad_qkv,
         grad_proj,
-        sums_dense[:width],
-        sums_dense[width:],
+        sums_up,
+        sums_down,
         router_grad,
         grad_ex_up.astype(f32)[None],
         grad_ex_down.astype(f32)[None],

time: 920 us -> 747 us (0.81)
  local copies, waits for them, and re-layouts: 136 us -> 47.7 us
  waiting for transfers between devices: 448 us -> 394 us
  matrix products: 182 us -> 131 us
  Pallas kernels: 0 us -> 28 us
  starting transfers between devices: 63.2 us -> 87.2 us
  other arithmetic: 64.5 us -> 48.7 us
  between operations: 16.9 us -> 4.12 us
    psum x3 -> x0, waiting for transfers between devices: 167 us -> none  [total(): return lax.psum(jnp.concatenate(parts, axis=0), 'dp').astype(f32)]
    ppermute x0 -> x24, waiting for transfers between devices: none -> 120 us  [dp_flip(): lax.ppermute(values, 'dp', [(i, i ^ 1 << bit) for i in range(groups)])]
    squeeze x12 -> x0, local copies, waits for them, and re-layouts: 32.6 us -> none  [attention_forward(): queries, key_rows, value_rows = (rounded[0], rounded[1], rounded[2])]
    ppermute x0 -> x24, starting transfers between devices: none -> 28.4 us  [dp_flip(): lax.ppermute(values, 'dp', [(i, i ^ 1 << bit) for i in range(groups)])]
    pallas_call x0 -> x4, Pallas kernels: none -> 28 us  [the longest x2 20.2 us: attend_grad(): pl.pallas_call(context_grad_kernel, grid=(images,), in_specs=[pl.BlockSpe...]
    dot_general x12 -> x0, matrix products: 24.9 us -> none  [the longest x2 7.7 us: attention_backward(): jnp.einsum('ishd,ithd->ihst', grad_context, value_rows, preferred_element...]
    another operation x19 -> x1, local copies, waits for them, and re-layouts: 21.1 us -> 0.02 us  [the longest x14 19.2 us: attention_backward(): jnp.stack([grad_queries, grad_keys, grad_values]).astype(bf16)]
    reshape x6 -> x0, local copies, waits for them, and re-layouts: 11.2 us -> none  [the longest x4 8.5 us: attention_backward(): matmul_nt(grad_branch, proj_w).astype(bf16).reshape(queries.shape)]
  transfers between devices with their start and end apart: 77 -> 96, of which waited for: 28 -> 43; matrix products, arithmetic and copies ran while one was open for 27% -> 22% of each run, Pallas kernels for 0% -> 2%
where the time goes in v2:
time: 747 us; the launch traced here: 740 us
  waiting for transfers between devices  394 us (53%)
  matrix products  131 us (18%)
  starting transfers between devices  87.2 us (12%)
  other arithmetic  48.7 us (7%)
  local copies, waits for them, and re-layouts  47.7 us (6%)
  Pallas kernels  28 us (4%)
    ppermute x68, waiting for transfers between devices, flip(): return lax.ppermute(values, 'tensor', [(i, i ^ mask) for i in range(ranks)])  228 us
    ppermute x24, waiting for transfers between devices, dp_flip(): lax.ppermute(values, 'dp', [(i, i ^ 1 << bit) for i in range(groups)])  120 us
    all_to_all x4, waiting for transfers between devices, all_to_all(): lax.all_to_all(split_rows, 'dp', split_axis=0, concat_axis=0, tiled=True)  45.5 us
    ppermute x68, starting transfers between devices, flip(): return lax.ppermute(values, 'tensor', [(i, i ^ mask) for i in range(ranks)])  39.2 us
    dot_general x8, matrix products, matmul_tn(): lax.dot_general(left_side, right_side, (((0,), (0,)), ((), ())), preferre...  38 us
    dot_general x8, matrix products, matmul(): return jnp.dot(left_side, right_side, preferred_element_type=f32)  36.6 us
    dot_general x6, matrix products, matmul_nt(): lax.dot_general(left_side, right_side, (((1,), (1,)), ((), ())), preferre...  33.8 us
    ppermute x24, starting transfers between devices, dp_flip(): lax.ppermute(values, 'dp', [(i, i ^ 1 << bit) for i in range(groups)])  28.4 us
  transfers between devices with their start and end apart: 96, of which 43 were waited for; matrix products, arithmetic and copies ran while one was open for 22% of the time, Pallas kernels for 2%

profile of v2, /device:TPU:0, one launch (start us, length us, event | category | flops | bytes accessed | tf_op | source)
XLA Modules:
  0.0 740.3 jit_solution(16210509224459702082)
XLA Ops:
  16.9 9.6 %collective-permute-done.1 = bf16[3,192,768]{2,1,0:T(8,128)(2,1)} collective-permute-done((bf16[3,192,768]{2,1,0:T(8,128)(2,1)}, bf16[3,192,768]{2,1,0:T(8,128)(2,1)}, u32[]{:S(2)}, u32[]{:S(2)}) %collective-permute-start.1) | collective-permute-done | bytes 884768 | tf_op jit(solution)/shard_map/ppermute | solution.py:36
  43.0 18.2 %collective-permute-done.7 = bf16[768,768]{1,0:T(8,128)(2,1)} collective-permute-done((bf16[768,768]{1,0:T(8,128)(2,1)}, bf16[768,768]{1,0:T(8,128)(2,1)}, u32[]{:S(2)}, u32[]{:S(2)}) %collective-permute-start.7) | collective-permute-done | bytes 1179680 | tf_op jit(solution)/shard_map/ppermute | solution.py:36
  71.7 18.2 %collective-permute-done.10 = bf16[768,768]{1,0:T(8,128)(2,1)S(1)} collective-permute-done((bf16[768,768]{1,0:T(8,128)(2,1)}, bf16[768,768]{1,0:T(8,128)(2,1)S(1)}, u32[]{:S(2)}, u32[]{:S(2)}) %collective-permute-start.10) | collective-permute-done | bytes 1179680 | tf_op jit(solution)/shard_map/ppermute | solution.py:36
  95.1 16.9 %collective-permute-done.13 = bf16[3,192,768]{2,1,0:T(8,128)(2,1)S(1)} collective-permute-done((bf16[3,192,768]{2,1,0:T(8,128)(2,1)S(1)}, bf16[3,192,768]{2,1,0:T(8,128)(2,1)S(1)}, u32[]{:S(2)}, u32[]{:S(2)}) %collective-permute-start.13) | collective-permute-done | bytes 884768 | tf_op jit(solution)/shard_map/ppermute | solution.py:36
  134.6 12.3 %collective-permute-done.19 = bf16[416,768]{1,0:T(8,128)(2,1)} collective-permute-done((bf16[416,768]{1,0:T(8,128)(2,1)}, bf16[416,768]{1,0:T(8,128)(2,1)}, u32[]{:S(2)}, u32[]{:S(2)}) %collective-permute-start.19) | collective-permute-done | bytes 639008 | tf_op jit(solution)/shard_map/ppermute | solution.py:36
  160.6 15.4 %collective-permute-done.22 = bf16[768,768]{1,0:T(8,128)(2,1)} collective-permute-done((bf16[768,768]{1,0:T(8,128)(2,1)}, bf16[768,768]{1,0:T(8,128)(2,1)}, u32[]{:S(2)}, u32[]{:S(2)}) %collective-permute-start.22) | collective-permute-done | bytes 1179680 | tf_op jit(solution)/shard_map/ppermute | solution.py:36
  177.7 26.3 %collective-permute-done.25 = bf16[768,768]{1,0:T(8,128)(2,1)} collective-permute-done((bf16[768,768]{1,0:T(8,128)(2,1)}, bf16[768,768]{1,0:T(8,128)(2,1)}, u32[]{:S(2)}, u32[]{:S(2)}) %collective-permute-start.25) | collective-permute-done | bytes 1179680 | tf_op jit(solution)/shard_map/ppermute | solution.py:36
  204.0 6.9 fusion.44
  210.9 11.7 %convolution_convert_fusion.11 = bf16[832,768]{1,0:T(8,128)(2,1)} fusion(bf16[768,768]{1,0:T(8,128)(2,1)} %collective-permute-done.26, bf16[768,768]{1,0:T(8,128)(2,1)} %collective-permute-done.25, bf16[768,768]{1,0:T(8,128)(2,1)} %collective-permute-done.24, bf16[768,768]{1,0:T(8,128)(2,1)S(1)} %bitcast.193, f32[832,3072]{1,0:T(8,128)S(1)} %fusion.44), kind=kOutput, calls=%fused_computation.89 | convolution fusion | flops 3968385024 | bytes 16220160 | tf_op jit(solution)/shard_map/dot_general | solution.py:19
  234.4 25.4 %all-to-all-done.1 = bf16[8,104,768]{2,1,0:T(8,128)(2,1)} async-done(((bf16[8,104,768]{2,1,0:T(8,128)(2,1)}), bf16[8,104,768]{2,1,0:T(8,128)(2,1)}, u32[]{:S(2)}, u32[]{:S(2)}) %all-to-all-start.1) | async-done | bytes 1277984 | tf_op jit(solution)/shard_map/all_to_all | solution.py:287
  280.1 20.1 %all-to-all-done.2 = bf16[8,104,768]{2,1,0:T(8,128)(2,1)} async-done(((bf16[8,104,768]{2,1,0:T(8,128)(2,1)}), bf16[8,104,768]{2,1,0:T(8,128)(2,1)}, u32[]{:S(2)}, u32[]{:S(2)}) %all-to-all-start.2) | async-done | bytes 1277984 | tf_op jit(solution)/shard_map/all_to_all | solution.py:287
  300.2 10.0 %convolution_convert_fusion.2 = bf16[3072,768]{1,0:T(8,128)(2,1)S(1)} fusion(bf16[832,768]{1,0:T(8,128)(2,1)} %bitcast.25, f32[832,3072]{1,0:T(8,128)} %copy-done.76), kind=kOutput, calls=%fused_computation.30 | convolution fusion | flops 3951230976 | bytes 16220160 | tf_op jit(solution)/shard_map/dot_general | solution.py:23
  313.6 15.2 %fusion.6 = bf16[832,3072]{1,0:T(8,128)(2,1)S(1)} fusion(f32[832,3072]{1,0:T(8,128)} %copy-done.76, bf16[832,768]{1,0:T(8,128)(2,1)} %bitcast.25, bf16[768,768]{1,0:T(8,128)(2,1)} %collective-permute-done.26, bf16[768,768]{1,0:T(8,128)(2,1)} %collective-permute-done.25, bf16[768,768]{1,0:T(8,128)(2,1)} %collective-permute-done.24, ...), kind=kOutput, calls=%fused_computation.8 | convolution fusion | flops 3995860992 | bytes 21331968 | tf_op jit(solution)/shard_map/dot_general | solution.py:29
  328.8 9.0 %convolution_convert_fusion.10 = bf16[832,768]{1,0:T(8,128)(2,1)} fusion(bf16[832,3072]{1,0:T(8,128)(2,1)S(1)} %fusion.6, bf16[768,768]{1,0:T(8,128)(2,1)} %collective-permute-done.23, bf16[768,768]{1,0:T(8,128)(2,1)} %collective-permute-done.22, bf16[768,768]{1,0:T(8,128)(2,1)} %collective-permute-done.21, bf16[768,768]{1,0:T(8,128)(2,1)S(1)} %bitcast.198), kind=kOutput, calls=%fused_computation.88 | convolution fusion | flops 3945381888 | bytes 11108352 | tf_op jit(solution)/shard_map/dot_general | solution.py:29
  341.5 7.6 %convolution_convert_fusion.3 = bf16[768,3072]{1,0:T(8,128)(2,1)S(1)} fusion(bf16[832,768]{1,0:T(8,128)(2,1)} %bitcast.18, bf16[832,3072]{1,0:T(8,128)(2,1)} %copy-done.75), kind=kOutput, calls=%fused_computation.31 | convolution fusion | flops 3928227840 | bytes 11108352 | tf_op jit(solution)/shard_map/dot_general | solution.py:23
  360.6 19.3 %collective-permute-done.33 = bf16[768,768]{1,0:T(8,128)(2,1)S(1)} collective-permute-done((bf16[768,768]{1,0:T(8,128)(2,1)S(1)}, bf16[768,768]{1,0:T(8,128)(2,1)S(1)}, u32[]{:S(2)}, u32[]{:S(2)}) %collective-permute-start.33) | collective-permute-done | bytes 1179680 | tf_op jit(solution)/shard_map/ppermute | solution.py:36
  394.8 10.6 %collective-permute-done.36 = bf16[416,768]{1,0:T(8,128)(2,1)S(1)} collective-permute-done((bf16[416,768]{1,0:T(8,128)(2,1)S(1)}, bf16[416,768]{1,0:T(8,128)(2,1)S(1)}, u32[]{:S(2)}, u32[]{:S(2)}) %collective-permute-start.36) | collective-permute-done | bytes 639008 | tf_op jit(solution)/shard_map/ppermute | solution.py:36
  409.7 10.0 %shard_map.197 = bf16[3,2,208,768]{3,2,1,0:T(8,128)(2,1)S(1)} custom-call(bf16[3,2,208,768]{3,2,1,0:T(8,128)(2,1)S(1)} %bitcast.156, bf16[416,768]{1,0:T(8,128)(2,1)S(1)} %convolution_convert_fusion.15.grad_ref), custom_call_target="tpu_custom_call" | custom-call | flops 664535040 | bytes 4472832 | tf_op jit(solution)/shard_map/pallas_call | solution.py:203
  427.1 25.8 %collective-permute-done.51 = bf16[10,768]{1,0:T(8,128)(2,1)S(1)} collective-permute-done((bf16[10,768]{1,0:T(8,128)(2,1)S(1)}, bf16[10,768]{1,0:T(8,128)(2,1)S(1)}, u32[]{:S(2)}, u32[]{:S(2)}) %collective-permute-start.51) | collective-permute-done | bytes 15392 | tf_op jit(solution)/shard_map/ppermute | solution.py:36
  479.4 23.2 %collective-permute-done.49 = bf16[768,768]{1,0:T(8,128)(2,1)S(1)} collective-permute-done((bf16[768,768]{1,0:T(8,128)(2,1)S(1)}, bf16[768,768]{1,0:T(8,128)(2,1)S(1)}, u32[]{:S(2)}, u32[]{:S(2)}) %collective-permute-start.49) | collective-permute-done | bytes 1179680 | tf_op jit(solution)/shard_map/ppermute | solution.py:36
  510.6 10.2 %shard_map.198 = bf16[3,2,208,768]{3,2,1,0:T(8,128)(2,1)S(1)} custom-call(bf16[3,2,208,768]{3,2,1,0:T(8,128)(2,1)S(1)} %bitcast.154, bf16[416,768]{1,0:T(8,128)(2,1)S(1)} %convolution_convert_fusion.14.grad_ref), custom_call_target="tpu_custom_call" | custom-call | flops 664535040 | bytes 4472832 | tf_op jit(solution)/shard_map/pallas_call | solution.py:203
  523.1 9.7 %collective-permute-done.53 = bf16[768,768]{1,0:T(8,128)(2,1)S(1)} collective-permute-done((bf16[768,768]{1,0:T(8,128)(2,1)S(1)}, bf16[768,768]{1,0:T(8,128)(2,1)S(1)}, u32[]{:S(2)}, u32[]{:S(2)}) %collective-permute-start.53) | collective-permute-done | bytes 1179680 | tf_op jit(solution)/shard_map/ppermute | solution.py:36
  552.6 11.3 %collective-permute-done.68 = bf16[2,768]{1,0:T(2,128)(2,1)S(1)} collective-permute-done((bf16[2,768]{1,0:T(2,128)(2,1)S(1)}, bf16[2,768]{1,0:T(2,128)(2,1)S(1)}, u32[]{:S(2)}, u32[]{:S(2)}) %collective-permute-start.68) | collective-permute-done | bytes 3104 | tf_op jit(solution)/shard_map/ppermute | solution.py:36
  574.5 6.5 collective-permute-done.77
  588.7 9.3 %collective-permute-done.89 = bf16[96,768]{1,0:T(8,128)(2,1)S(1)} collective-permute-done((bf16[96,768]{1,0:T(8,128)(2,1)S(1)}, bf16[96,768]{1,0:T(8,128)(2,1)S(1)}, u32[]{:S(2)}, u32[]{:S(2)}) %collective-permute-start.89) | collective-permute-done | bytes 147488 | tf_op jit(solution)/shard_map/ppermute | solution.py:74
  609.8 8.1 %collective-permute-done.80 = bf16[384,768]{1,0:T(8,128)(2,1)S(1)} collective-permute-done((bf16[384,768]{1,0:T(8,128)(2,1)S(1)}, bf16[384,768]{1,0:T(8,128)(2,1)S(1)}, u32[]{:S(2)}, u32[]{:S(2)}) %collective-permute-start.80) | collective-permute-done | bytes 589856 | tf_op jit(solution)/shard_map/ppermute | solution.py:74
  619.3 12.3 %collective-permute-done.79 = bf16[416,768]{1,0:T(8,128)(2,1)S(1)} collective-permute-done((bf16[416,768]{1,0:T(8,128)(2,1)S(1)}, bf16[416,768]{1,0:T(8,128)(2,1)S(1)}, u32[]{:S(2)}, u32[]{:S(2)}) %collective-permute-start.79) | collective-permute-done | bytes 639008 | tf_op jit(solution)/shard_map/ppermute | solution.py:74
  639.3 9.2 %collective-permute-done.82 = bf16[96,768]{1,0:T(8,128)(2,1)S(1)} collective-permute-done((bf16[96,768]{1,0:T(8,128)(2,1)S(1)}, bf16[96,768]{1,0:T(8,128)(2,1)S(1)}, u32[]{:S(2)}, u32[]{:S(2)}) %collective-permute-start.82) | collective-permute-done | bytes 147488 | tf_op jit(solution)/shard_map/ppermute | solution.py:74
  665.1 6.9 collective-permute-done.69
  691.7 6.7 collective-permute-done.72
  698.8 9.1 %collective-permute-done.73 = bf16[208,768]{1,0:T(8,128)(2,1)S(1)} collective-permute-done((bf16[208,768]{1,0:T(8,128)(2,1)S(1)}, bf16[208,768]{1,0:T(8,128)(2,1)S(1)}, u32[]{:S(2)}, u32[]{:S(2)}) %collective-permute-start.73) | collective-permute-done | bytes 319520 | tf_op jit(solution)/shard_map/ppermute | solution.py:74
  718.1 6.5 collective-permute-done.74
  (577 shorter events, 318.9 us)
Async XLA Ops:
  6.5 54.7 %collective-permute-start = (bf16[3,192,768]{2,1,0:T(8,128)(2,1)}, bf16[3,192,768]{2,1,0:T(8,128)(2,1)}, u32[]{:S(2)}, u32[]{:S(2)}) collective-permute-start(bf16[3,192,768]{2,1,0:T(8,128)(2,1)} %get-tuple-element.130), channel_id=1, source_target_pairs={{0,1},{1,0},{2,3},{3,2},{4,5},{5,4},{6,7},{7,6},{8,9},{9,8},{10,11... | collective-permute-start | bytes 2654216 | tf_op jit(solution)/shard_map/ppermute | solution.py:36
  6.5 31.9 %collective-permute-start.6 = (bf16[768,768]{1,0:T(8,128)(2,1)}, bf16[768,768]{1,0:T(8,128)(2,1)}, u32[]{:S(2)}, u32[]{:S(2)}) collective-permute-start(bf16[768,768]{1,0:T(8,128)(2,1)} %param.19), channel_id=1, source_target_pairs={{0,1},{1,0},{2,3},{3,2},{4,5},{5,4},{6,7},{7,6},{8,9},{9,8},{10,11... | collective-permute-start | bytes 3538952 | tf_op jit(solution)/shard_map/ppermute | solution.py:36
  7.0 34.0 %collective-permute-start.9 = (bf16[768,768]{1,0:T(8,128)(2,1)}, bf16[768,768]{1,0:T(8,128)(2,1)}, u32[]{:S(2)}, u32[]{:S(2)}) collective-permute-start(bf16[768,768]{1,0:T(8,128)(2,1)} %param.20), channel_id=1, source_target_pairs={{0,1},{1,0},{2,3},{3,2},{4,5},{5,4},{6,7},{7,6},{8,9},{9,8},{10,11... | collective-permute-start | bytes 3538952 | tf_op jit(solution)/shard_map/ppermute | solution.py:36
  38.5 31.9 %collective-permute-start.3 = (bf16[192,768]{1,0:T(8,128)(2,1)S(1)}, bf16[192,768]{1,0:T(8,128)(2,1)S(1)}, u32[]{:S(2)}, u32[]{:S(2)}) collective-permute-start(bf16[192,768]{1,0:T(8,128)(2,1)S(1)} %get-tuple-element.40), channel_id=1, source_target_pairs={{0,1},{1,0},{2,3},{3,2},{4,5},{5,4},{6,7},{7,6},{8,9},{9,8},{10,11... | collective-permute-start | bytes 884744 | tf_op jit(solution)/shard_map/ppermute | solution.py:36
  41.1 79.8 %collective-permute-start.12 = (bf16[3,192,768]{2,1,0:T(8,128)(2,1)S(1)}, bf16[3,192,768]{2,1,0:T(8,128)(2,1)S(1)}, u32[]{:S(2)}, u32[]{:S(2)}) collective-permute-start(bf16[3,192,768]{2,1,0:T(8,128)(2,1)S(1)} %copy-done.25), channel_id=1, source_target_pairs={{0,1},{1,0},{2,3},{3,2},{4,5},{5,4},{6,7},{7,6},{8,9},{9,8},{10,11... | collective-permute-start | bytes 2654216 | tf_op jit(solution)/shard_map/ppermute | solution.py:36
  61.2 65.6 %collective-permute-start.15 = (bf16[192,768]{1,0:T(8,128)(2,1)S(1)}, bf16[192,768]{1,0:T(8,128)(2,1)S(1)}, u32[]{:S(2)}, u32[]{:S(2)}) collective-permute-start(bf16[192,768]{1,0:T(8,128)(2,1)S(1)} %copy-done.35), channel_id=1, source_target_pairs={{0,1},{1,0},{2,3},{3,2},{4,5},{5,4},{6,7},{7,6},{8,9},{9,8},{10,11... | collective-permute-start | bytes 884744 | tf_op jit(solution)/shard_map/ppermute | solution.py:36
  61.8 28.2 %collective-permute-start.10 = (bf16[768,768]{1,0:T(8,128)(2,1)}, bf16[768,768]{1,0:T(8,128)(2,1)S(1)}, u32[]{:S(2)}, u32[]{:S(2)}) collective-permute-start(bf16[768,768]{1,0:T(8,128)(2,1)} %param.20), channel_id=1, source_target_pairs={{0,2},{1,3},{2,0},{3,1},{4,6},{5,7},{6,4},{7,5},{8,10},{9,11},{10,... | collective-permute-start | bytes 3538952 | tf_op jit(solution)/shard_map/ppermute | solution.py:36
  147.3 28.7 %collective-permute-start.22 = (bf16[768,768]{1,0:T(8,128)(2,1)}, bf16[768,768]{1,0:T(8,128)(2,1)}, u32[]{:S(2)}, u32[]{:S(2)}) collective-permute-start(bf16[768,768]{1,0:T(8,128)(2,1)} %bitcast.195), channel_id=1, source_target_pairs={{0,2},{1,3},{2,0},{3,1},{4,6},{5,7},{6,4},{7,5},{8,10},{9,11},{10,... | collective-permute-start | bytes 3538952 | tf_op jit(solution)/shard_map/ppermute | solution.py:36
  155.0 49.0 %all-to-all-start = ((bf16[8,104,768]{2,1,0:T(8,128)(2,1)}), bf16[8,104,768]{2,1,0:T(8,128)(2,1)}, u32[]{:S(2)}, u32[]{:S(2)}) async-start(bf16[8,104,768]{2,1,0:T(8,128)(2,1)} %bitcast.176), calls=%async_computation | async-start | bytes 2555904 | tf_op jit(solution)/shard_map/all_to_all | solution.py:287
  177.7 33.2 %collective-permute-start.24 = (bf16[768,768]{1,0:T(8,128)(2,1)}, bf16[768,768]{1,0:T(8,128)(2,1)}, u32[]{:S(2)}, u32[]{:S(2)}) collective-permute-start(bf16[768,768]{1,0:T(8,128)(2,1)} %bitcast.192), channel_id=1, source_target_pairs={{0,1},{1,0},{2,3},{3,2},{4,5},{5,4},{6,7},{7,6},{8,9},{9,8},{10,11... | collective-permute-start | bytes 3538952 | tf_op jit(solution)/shard_map/ppermute | solution.py:36
  222.6 37.2 %all-to-all-start.1 = ((bf16[8,104,768]{2,1,0:T(8,128)(2,1)}), bf16[8,104,768]{2,1,0:T(8,128)(2,1)}, u32[]{:S(2)}, u32[]{:S(2)}) async-start(bf16[8,104,768]{2,1,0:T(8,128)(2,1)} %bitcast.175), calls=%async_computation.1 | async-start | bytes 2555904 | tf_op jit(solution)/shard_map/all_to_all | solution.py:287
  265.2 35.0 %all-to-all-start.2 = ((bf16[8,104,768]{2,1,0:T(8,128)(2,1)}), bf16[8,104,768]{2,1,0:T(8,128)(2,1)}, u32[]{:S(2)}, u32[]{:S(2)}) async-start(bf16[8,104,768]{2,1,0:T(8,128)(2,1)} %bitcast.172), calls=%async_computation.2 | async-start | bytes 2555904 | tf_op jit(solution)/shard_map/all_to_all | solution.py:287
  272.1 83.2 %collective-permute-start.38 = (f32[832]{0:T(1024)S(1)}, f32[832]{0:T(1024)S(1)}, u32[]{:S(2)}, u32[]{:S(2)}) collective-permute-start(f32[832]{0:T(1024)S(1)} %get-tuple-element.128), channel_id=1, source_target_pairs={{0,2},{1,3},{2,0},{3,1},{4,6},{5,7},{6,4},{7,5},{8,10},{9,11},{10,... | collective-permute-start | bytes 9992 | tf_op jit(solution)/shard_map/ppermute | solution.py:36
  313.1 36.7 %collective-permute-start.32 = (bf16[768,768]{1,0:T(8,128)(2,1)}, bf16[768,768]{1,0:T(8,128)(2,1)}, u32[]{:S(2)}, u32[]{:S(2)}) collective-permute-start(bf16[768,768]{1,0:T(8,128)(2,1)} %get-tuple-element.102), channel_id=1, source_target_pairs={{0,1},{1,0},{2,3},{3,2},{4,5},{5,4},{6,7},{7,6},{8,9},{9,8},{10,11... | collective-permute-start | bytes 3538952 | tf_op jit(solution)/shard_map/ppermute | solution.py:36
  313.1 47.4 %collective-permute-start.31 = (bf16[768,768]{1,0:T(8,128)(2,1)}, bf16[768,768]{1,0:T(8,128)(2,1)}, u32[]{:S(2)}, u32[]{:S(2)}) collective-permute-start(bf16[768,768]{1,0:T(8,128)(2,1)} %get-tuple-element.101), channel_id=1, source_target_pairs={{0,1},{1,0},{2,3},{3,2},{4,5},{5,4},{6,7},{7,6},{8,9},{9,8},{10,11... | collective-permute-start | bytes 3538952 | tf_op jit(solution)/shard_map/ppermute | solution.py:36
  337.9 45.1 %all-to-all-start.3 = ((bf16[8,104,768]{2,1,0:T(8,128)(2,1)}), bf16[8,104,768]{2,1,0:T(8,128)(2,1)S(1)}, u32[]{:S(2)}, u32[]{:S(2)}) async-start(bf16[8,104,768]{2,1,0:T(8,128)(2,1)} %bitcast.174), calls=%async_computation.3 | async-start | bytes 2555904 | tf_op jit(solution)/shard_map/all_to_all | solution.py:287
  352.0 27.9 %collective-permute-start.33 = (bf16[768,768]{1,0:T(8,128)(2,1)S(1)}, bf16[768,768]{1,0:T(8,128)(2,1)S(1)}, u32[]{:S(2)}, u32[]{:S(2)}) collective-permute-start(bf16[768,768]{1,0:T(8,128)(2,1)S(1)} %add_convert_fusion.10), channel_id=1, source_target_pairs={{0,2},{1,3},{2,0},{3,1},{4,6},{5,7},{6,4},{7,5},{8,10},{9,11},{10,... | collective-permute-start | bytes 3538952 | tf_op jit(solution)/shard_map/ppermute | solution.py:36
  357.6 34.3 %collective-permute-start.28 = (bf16[416,768]{1,0:T(8,128)(2,1)}, bf16[416,768]{1,0:T(8,128)(2,1)}, u32[]{:S(2)}, u32[]{:S(2)}) collective-permute-start(bf16[416,768]{1,0:T(8,128)(2,1)} %get-tuple-element.124), channel_id=1, source_target_pairs={{0,1},{1,0},{2,3},{3,2},{4,5},{5,4},{6,7},{7,6},{8,9},{9,8},{10,11... | collective-permute-start | bytes 1916936 | tf_op jit(solution)/shard_map/ppermute | solution.py:36
  424.0 31.4 %collective-permute-start.44 = (bf16[768,768]{1,0:T(8,128)(2,1)S(1)}, bf16[768,768]{1,0:T(8,128)(2,1)S(1)}, u32[]{:S(2)}, u32[]{:S(2)}) collective-permute-start(bf16[768,768]{1,0:T(8,128)(2,1)S(1)} %copy-done.24), channel_id=1, source_target_pairs={{0,2},{1,3},{2,0},{3,1},{4,6},{5,7},{6,4},{7,5},{8,10},{9,11},{10,... | collective-permute-start | bytes 3538952 | tf_op jit(solution)/shard_map/ppermute | solution.py:36
  425.7 29.0 %collective-permute-start.40 = (bf16[3,192,768]{2,1,0:T(8,128)(2,1)S(1)}, bf16[3,192,768]{2,1,0:T(8,128)(2,1)S(1)}, u32[]{:S(2)}, u32[]{:S(2)}) collective-permute-start(bf16[3,192,768]{2,1,0:T(8,128)(2,1)S(1)} %get-tuple-element.114), channel_id=1, source_target_pairs={{0,1},{1,0},{2,3},{3,2},{4,5},{5,4},{6,7},{7,6},{8,9},{9,8},{10,11... | collective-permute-start | bytes 2654216 | tf_op jit(solution)/shard_map/ppermute | solution.py:36
  425.9 28.7 %collective-permute-start.42 = (bf16[3,192,768]{2,1,0:T(8,128)(2,1)S(1)}, bf16[3,192,768]{2,1,0:T(8,128)(2,1)S(1)}, u32[]{:S(2)}, u32[]{:S(2)}) collective-permute-start(bf16[3,192,768]{2,1,0:T(8,128)(2,1)S(1)} %get-tuple-element.113), channel_id=1, source_target_pairs={{0,1},{1,0},{2,3},{3,2},{4,5},{5,4},{6,7},{7,6},{8,9},{9,8},{10,11... | collective-permute-start | bytes 2654216 | tf_op jit(solution)/shard_map/ppermute | solution.py:36
  474.3 28.3 %collective-permute-start.49 = (bf16[768,768]{1,0:T(8,128)(2,1)S(1)}, bf16[768,768]{1,0:T(8,128)(2,1)S(1)}, u32[]{:S(2)}, u32[]{:S(2)}) collective-permute-start(bf16[768,768]{1,0:T(8,128)(2,1)S(1)} %pad_maximum_fusion.11), channel_id=1, source_target_pairs={{0,2},{1,3},{2,0},{3,1},{4,6},{5,7},{6,4},{7,5},{8,10},{9,11},{10,... | collective-permute-start | bytes 3538952 | tf_op jit(solution)/shard_map/ppermute | solution.py:36
  502.6 187.1 %collective-permute-start.27 = (bf16[416,768]{1,0:T(8,128)(2,1)S(1)}, bf16[416,768]{1,0:T(8,128)(2,1)S(1)}, u32[]{:S(2)}, u32[]{:S(2)}) collective-permute-start(bf16[416,768]{1,0:T(8,128)(2,1)S(1)} %copy-done.27), channel_id=1, source_target_pairs={{0,1},{1,0},{2,3},{3,2},{4,5},{5,4},{6,7},{7,6},{8,9},{9,8},{10,11... | collective-permute-start | bytes 1916936 | tf_op jit(solution)/shard_map/ppermute | solution.py:36
  504.3 28.4 %collective-permute-start.53 = (bf16[768,768]{1,0:T(8,128)(2,1)S(1)}, bf16[768,768]{1,0:T(8,128)(2,1)S(1)}, u32[]{:S(2)}, u32[]{:S(2)}) collective-permute-start(bf16[768,768]{1,0:T(8,128)(2,1)S(1)} %get-tuple-element.58), channel_id=1, source_target_pairs={{0,2},{1,3},{2,0},{3,1},{4,6},{5,7},{6,4},{7,5},{8,10},{9,11},{10,... | collective-permute-start | bytes 3538952 | tf_op jit(solution)/shard_map/ppermute | solution.py:36
  536.8 64.5 %collective-permute-start.58 = (bf16[768,768]{1,0:T(8,128)(2,1)S(1)}, bf16[768,768]{1,0:T(8,128)(2,1)S(1)}, u32[]{:S(2)}, u32[]{:S(2)}) collective-permute-start(bf16[768,768]{1,0:T(8,128)(2,1)S(1)} %get-tuple-element.63), channel_id=1, source_target_pairs={{0,2},{1,3},{2,0},{3,1},{4,6},{5,7},{6,4},{7,5},{8,10},{9,11},{10,... | collective-permute-start | bytes 3538952 | tf_op jit(solution)/shard_map/ppermute | solution.py:36
  546.1 41.0 %collective-permute-start.54 = (bf16[3,192,768]{2,1,0:T(8,128)(2,1)S(1)}, bf16[3,192,768]{2,1,0:T(8,128)(2,1)S(1)}, u32[]{:S(2)}, u32[]{:S(2)}) collective-permute-start(bf16[3,192,768]{2,1,0:T(8,128)(2,1)S(1)} %get-tuple-element.109), channel_id=1, source_target_pairs={{0,1},{1,0},{2,3},{3,2},{4,5},{5,4},{6,7},{7,6},{8,9},{9,8},{10,11... | collective-permute-start | bytes 2654216 | tf_op jit(solution)/shard_map/ppermute | solution.py:36
  587.0 111.5 %collective-permute-start.65 = (bf16[416,768]{1,0:T(8,128)(2,1)S(1)}, bf16[416,768]{1,0:T(8,128)(2,1)S(1)}, u32[]{:S(2)}, u32[]{:S(2)}) collective-permute-start(bf16[416,768]{1,0:T(8,128)(2,1)S(1)} %add_convert_fusion.21), channel_id=1, source_target_pairs={{0,1},{1,0},{2,3},{3,2},{4,5},{5,4},{6,7},{7,6},{8,9},{9,8},{10,11... | collective-permute-start | bytes 1916936 | tf_op jit(solution)/shard_map/ppermute | solution.py:36
  602.9 28.7 %collective-permute-start.79 = (bf16[416,768]{1,0:T(8,128)(2,1)S(1)}, bf16[416,768]{1,0:T(8,128)(2,1)S(1)}, u32[]{:S(2)}, u32[]{:S(2)}) collective-permute-start(bf16[416,768]{1,0:T(8,128)(2,1)S(1)} %pad_maximum_fusion.21), channel_id=1, source_target_pairs={{0,4},{4,0},{8,12},{12,8},{16,20},{20,16},{24,28},{28,24},{1,5},{5... | collective-permute-start | bytes 1916936 | tf_op jit(solution)/shard_map/ppermute | solution.py:74
  608.1 48.0 %collective-permute-start.59 = (bf16[768,768]{1,0:T(8,128)(2,1)S(1)}, bf16[768,768]{1,0:T(8,128)(2,1)S(1)}, u32[]{:S(2)}, u32[]{:S(2)}) collective-permute-start(bf16[768,768]{1,0:T(8,128)(2,1)S(1)} %pad_maximum_fusion.12), channel_id=1, source_target_pairs={{0,2},{1,3},{2,0},{3,1},{4,6},{5,7},{6,4},{7,5},{8,10},{9,11},{10,... | collective-permute-start | bytes 3538952 | tf_op jit(solution)/shard_map/ppermute | solution.py:36
  617.9 39.9 %collective-permute-start.91 = (bf16[384,768]{1,0:T(8,128)(2,1)S(1)}, bf16[384,768]{1,0:T(8,128)(2,1)S(1)}, u32[]{:S(2)}, u32[]{:S(2)}) collective-permute-start(bf16[384,768]{1,0:T(8,128)(2,1)S(1)} %pad_maximum_fusion.27), channel_id=1, source_target_pairs={{0,4},{4,0},{8,12},{12,8},{16,20},{20,16},{24,28},{28,24},{1,5},{5... | collective-permute-start | bytes 1769480 | tf_op jit(solution)/shard_map/ppermute | solution.py:74
  690.1 28.0 %collective-permute-start.63 = (bf16[416,768]{1,0:T(8,128)(2,1)S(1)}, bf16[416,768]{1,0:T(8,128)(2,1)}, u32[]{:S(2)}, u32[]{:S(2)}) collective-permute-start(bf16[416,768]{1,0:T(8,128)(2,1)S(1)} %add_convert_fusion.19), channel_id=1, source_target_pairs={{0,2},{1,3},{2,0},{3,1},{4,6},{5,7},{6,4},{7,5},{8,10},{9,11},{10,... | collective-permute-start | bytes 1916936 | tf_op jit(solution)/shard_map/ppermute | solution.py:36
  691.7 41.0 %collective-permute-start.62 = (bf16[416,768]{1,0:T(8,128)(2,1)S(1)}, bf16[416,768]{1,0:T(8,128)(2,1)}, u32[]{:S(2)}, u32[]{:S(2)}) collective-permute-start(bf16[416,768]{1,0:T(8,128)(2,1)S(1)} %add_convert_fusion.19), channel_id=1, source_target_pairs={{0,1},{1,0},{2,3},{3,2},{4,5},{5,4},{6,7},{7,6},{8,9},{9,8},{10,11... | collective-permute-start | bytes 1916936 | tf_op jit(solution)/shard_map/ppermute | solution.py:36
  (149 other events, 1809.8 us)

commit v3 on v2

--- a/solution.py
+++ b/solution.py
@@ -111,8 +111,12 @@
 
 def dp_rows(*parts):
     rows = jnp.concatenate(parts, axis=0)
-    unit = 8 * lax.axis_size("dp")
+    unit = 16 * lax.axis_size("dp")
     return jnp.pad(rows, ((0, -rows.shape[0] % unit), (0, 0)))
+
+
+def join(*values):
+    return lax.optimization_barrier(values)
 
 
 def norm_forward(values, norm_gain):
@@ -242,29 +246,6 @@
     return (grad_stream + grad_in, grad_qkv.astype(bf16), grad_proj.astype(bf16), grad_gain)
 
 
-def dense_forward(stream, norm_gain, up_w, down_w):
-    normed, unit_rows, inverse = norm_forward(stream, norm_gain)
-    normed_b = normed.astype(bf16)
-    hidden_pre = matmul(normed_b, up_w)
-    hidden_b = jax.nn.gelu(hidden_pre).astype(bf16)
-    return (
-        stream + matmul(hidden_b, down_w),
-        (unit_rows, inverse, normed_b, hidden_pre, hidden_b),
-    )
-
-
-def dense_backward(grad_stream, norm_gain, up_w, down_w, saved_state):
-    unit_rows, inverse, normed_b, hidden_pre, hidden_b = saved_state
-    grad_branch = grad_stream.astype(bf16)
-    grad_down = matmul_tn(hidden_b, grad_branch)
-    unused_out, gelu_back = jax.vjp(jax.nn.gelu, hidden_pre)
-    grad_pre = gelu_back(matmul_nt(grad_branch, down_w))[0].astype(bf16)
-    grad_up = matmul_tn(normed_b, grad_pre)
-    grad_normed = matmul_nt(grad_pre, up_w)
-    grad_in, grad_gain = norm_backward(grad_normed, norm_gain, unit_rows, inverse)
-    return (grad_stream + grad_in, grad_up.astype(bf16), grad_down.astype(bf16), grad_gain)
-
-
 def row_parts(values, axis):
     return jnp.split(values, lax.axis_size("tensor"), axis=axis)
 
@@ -323,24 +304,19 @@
     def own_of(whole):
         return lax.dynamic_slice_in_dim(whole, me * own_rows, own_rows, 0)
 
+    bits = dp_bits()
     qkv_t = jnp.swapaxes(attn_qkv, 2, 3)
+    columns = qkv_t.shape[2]
     far_qkv0 = far(qkv_t[0])
     far_proj0 = far(attn_proj[0], far_qkv0)
-    far_up = far(dense_up, far_proj0)
-    far_down = far(dense_down, far_up)
-    far_qkv1 = far(qkv_t[1], far_down)
-    far_proj1 = far(attn_proj[1], far_qkv1)
-    far_ex_up = far(expert_up[0], far_proj1)
+    far_qkv1 = far(qkv_t[1], far_qkv0)
     qkv0 = jnp.concatenate(near(qkv_t[0], far_qkv0), axis=1)
+    far_proj0 = after(far_proj0, qkv0)
     proj0 = jnp.concatenate(near(attn_proj[0], far_proj0), axis=0)
-    up_w = jnp.concatenate(near(dense_up, far_up), axis=1)
-    down_w = jnp.concatenate(near(dense_down, far_down), axis=0)
-    qkv1 = jnp.concatenate(near(qkv_t[1], far_qkv1), axis=1)
-    proj1 = jnp.concatenate(near(attn_proj[1], far_proj1), axis=0)
 
     capacity = (2 * tokens + experts - 1) // experts + 2
     quota = -(-capacity // ranks)
-    room = -(-quota // 8) * 8
+    room = -(-(quota + 3) // 8) * 8
     slots = experts * room
     rank = slots_of(expert_routes, image_count)
     holder = jnp.where(rank < 0, -1, rank // quota)
@@ -364,45 +340,83 @@
     stream0 = to_padded(own_of(image_tokens)).astype(f32)
     grad_out = to_padded(own_of(out_cotangent)).astype(f32)
     stream1, attn0_state = attention_forward(stream0, norm_gains[0, 0], qkv0, proj0)
-    stream2, dense_state = dense_forward(stream1, norm_gains[0, 1], up_w, down_w)
+    stream1, far_qkv1 = join(stream1, far_qkv1)
+
+    normed_m, dense_unit, dense_inverse = norm_forward(stream1, norm_gains[0, 1])
+    normed_m = normed_m.astype(bf16)
+    far_normed_m = far(normed_m)
+    cot_slot = matmul(pick_whole, out_cotangent)
+    far_normed_m, cot_slot = join(far_normed_m, cot_slot)
+    cot_in = all_to_all(cot_slot.astype(bf16))
+    normed_m = jnp.concatenate(near(normed_m, far_normed_m), axis=0)
+    dense_pre = matmul(normed_m, dense_up)
+    dense_hidden = jax.nn.gelu(dense_pre).astype(bf16)
+    dense_pair = near_sum(row_parts(matmul(dense_hidden, dense_down).astype(bf16), 0))
+    dense_sum = far_sum(dense_pair)
+    far_proj1 = far(attn_proj[1], dense_sum)
+    half = expert_up.shape[1] // 2
+    far_ex_up = far(expert_up[0, :half], far_proj1)
+    stream2 = stream1 + dense_sum.astype(f32)
+    qkv1 = jnp.concatenate(near(qkv_t[1], far_qkv1), axis=1)
+    proj1 = jnp.concatenate(near(attn_proj[1], far_proj1), axis=0)
     stream3, attn1_state = attention_forward(stream2, norm_gains[1, 0], qkv1, proj1)
 
+    stream3, cot_in, far_ex_up = join(stream3, cot_in, far_ex_up)
     normed, unit_rows, inverse = norm_forward(stream3, norm_gains[1, 1])
     normed_b = normed.astype(bf16)
     far_normed = far(normed_b)
-    normed_all = jnp.concatenate(near(normed_b, far_normed), axis=0)
-    far_ex_down = far(expert_down[0], (far_normed, far_ex_up))
-    ex_up = jnp.concatenate(near(expert_up[0], far_ex_up), axis=1)
-    ex_down = jnp.concatenate(near(expert_down[0], far_ex_down), axis=0)
-
-    rows_in = all_to_all(matmul(pick, normed_all).astype(bf16))
-    logits = jnp.dot(normed_all.astype(f32), router_weight, precision=highest)
-    gate_all = jax.nn.softmax(logits, axis=-1)
-    gate_probs = gate_all[:block]
-    routes_rel = blocked(expert_routes).reshape(2, ranks * block)
+    logits = jnp.dot(normed_b.astype(f32), router_weight, precision=highest)
+    gate_probs = jax.nn.softmax(logits, axis=-1)
+    gate_all = jnp.stack(gather(gate_probs.T))
+    routes_rel = blocked(expert_routes)
     expert_ids = jnp.arange(experts, dtype=jnp.int32)
-    chosen_rel = routes_rel[..., None] == expert_ids
-    gates = jnp.sum(jnp.where(chosen_rel, gate_all[None], 0.0), axis=-1)
+    gates = jnp.sum(
+        jnp.where(routes_rel[:, :, None] == expert_ids[:, None], gate_all[None], 0.0), axis=2
+    ).reshape(2, ranks * block)
     gate_slot = jnp.sum(
         jnp.where(first, gates[0], 0.0) + jnp.where(second, gates[1], 0.0), axis=1
-    )[:, None]
-    cot_slot = matmul(pick_whole, out_cotangent)
-    grad_rows = all_to_all((gate_slot * cot_slot).astype(bf16))
+    )
+    parts, left = [], gate_slot
+    for _ in range(3):
+        parts.append(lax.optimization_barrier(left.astype(bf16)))
+        left = left - parts[-1].astype(f32)
+    far_ex_up_rest = far(expert_up[0, half:], far_normed)
+    far_normed, gate_slot, parts = join(far_normed, gate_slot, parts)
+    normed_all = jnp.concatenate(near(normed_b, far_normed), axis=0)
+    far_ex_down = far(expert_down[0], far_ex_up_rest)
+    far_ex_up = jnp.concatenate([far_ex_up, far_ex_up_rest], axis=0)
+    send = matmul(pick, normed_all).astype(bf16).reshape(experts, room, width)
+    row = jnp.arange(room, dtype=jnp.int32)[:, None]
+    for at, part in enumerate(parts):
+        lanes = jnp.pad(part.reshape(experts, 1, room), ((0, 0), (0, 0), (0, width - room)))
+        send = jnp.where(row == quota + at, lanes, send)
+    rows_in = all_to_all(send.reshape(slots, width))
+    ex_up = jnp.concatenate(near(expert_up[0], far_ex_up), axis=1)
+    rows_in, ex_up = join(rows_in, ex_up)
+    ex_down = jnp.concatenate(near(expert_down[0], far_ex_down), axis=0)
+    gate_rows = rows_in.reshape(experts, room, width)[:, quota : quota + 3, :room]
+    gate_in = jnp.sum(gate_rows.astype(f32), axis=1).reshape(slots, 1)
+    grad_rows = (gate_in * cot_in.astype(f32)).astype(bf16)
 
     hidden_pre = matmul(rows_in, ex_up)
     hidden_b = jax.nn.gelu(hidden_pre).astype(bf16)
-    rows_out = all_to_all(matmul(hidden_b, ex_down).astype(bf16))
+    send_out = matmul(hidden_b, ex_down).astype(bf16)
+    rows_out = all_to_all(send_out)
     unused_out, gelu_back = jax.vjp(jax.nn.gelu, hidden_pre)
     grad_pre = gelu_back(matmul_nt(grad_rows, ex_down))[0].astype(bf16)
-    grad_back = all_to_all(matmul_nt(grad_pre, ex_up).astype(bf16))
-    down_pair = near_sum(row_parts(matmul_tn(hidden_b, grad_rows).astype(bf16), 0))
+    late_rows = after(grad_rows, send_out)
+    down_pair = near_sum(row_parts(matmul_tn(hidden_b, late_rows).astype(bf16), 0))
+    grad_pre, rows_out, down_pair = join(grad_pre, rows_out, down_pair)
+    send_back = matmul_nt(grad_pre, ex_up).astype(bf16)
     grad_ex_down = far_sum(down_pair)
+    send_back, grad_pre = join(send_back, grad_pre)
+    grad_back = all_to_all(send_back)
+    grad_pre, grad_ex_down = join(grad_pre, grad_ex_down)
     up_pair = near_sum(row_parts(matmul_tn(rows_in, grad_pre).astype(bf16), 1))
-    grad_back, up_pair, grad_ex_down = lax.optimization_barrier((grad_back, up_pair, grad_ex_down))
 
     out_f = rows_out.astype(f32)
     gate_grad_slot = jnp.sum(cot_slot * out_f, axis=1)
-    branch = matmul_tn(pick, (gate_slot * out_f).astype(bf16)).astype(bf16)
+    branch = matmul_tn(pick, (gate_slot[:, None] * out_f).astype(bf16)).astype(bf16)
 
     own_holder = blocked(holder)[:, 0]
     own_place = blocked(place)[:, 0]
@@ -419,9 +433,9 @@
         grad_probs - jnp.sum(gate_probs * grad_probs, axis=-1, keepdims=True)
     )
     grad_router = jnp.dot(normed_b.astype(f32).T, grad_logits, precision=highest)
+    grad_back, grad_logits, branch, ex_up_pair = join(grad_back, grad_logits, branch, up_pair)
     grad_branch = matmul_tn(pick, grad_back).astype(bf16)
     grad_normed = far_sum(near_sum(row_parts(grad_branch, 0)))
-    grad_ex_up = far_sum(up_pair, grad_normed)
     grad_normed = grad_normed.astype(f32) + jnp.dot(grad_logits, router_weight.T, precision=highest)
     grad_in, gain_expert = norm_backward(grad_normed, norm_gains[1, 1], unit_rows, inverse)
     grad3 = grad_out + grad_in
@@ -431,64 +445,87 @@
         values = add_rounded(values, flip(values, 1))
         return add_rounded(values, flip(values, 2))
 
-    columns = attn_qkv.shape[3]
-    bits = dp_bits()
-
-    def attn_pair(grad_qkv, grad_proj):
-        pairs = [near_sum(row_parts(grad_qkv, 1)), near_sum(row_parts(grad_proj, 0))]
+    def own_pair(*grads):
+        pairs = [near_sum(row_parts(one, axis)) for one, axis in grads]
         return tuple(
-            jnp.concatenate([qkv_part.reshape(-1, width), proj_part], axis=0)
-            for qkv_part, proj_part in zip(*pairs)
+            jnp.concatenate([one.reshape(-1, width) for one in side], axis=0)
+            for side in zip(*pairs)
         )
 
+    order_a = bits
+    order_b = [bits[1], bits[0]] + bits[2:]
+
+    def halve_both(pair, step):
+        return (dp_halve(pair[0], order_a[step]), dp_halve(pair[1], order_b[step]))
+
+    def double_both(pair, step):
+        return (dp_double(pair[0], order_a[step]), dp_double(pair[1], order_b[step]))
+
+    last = len(bits) - 1
     grad2, grad_qkv1, grad_proj1, gain_attn1 = attention_backward(
         grad3, norm_gains[1, 0], qkv1, proj1, attn1_state
     )
-    attn1_pair = attn_pair(grad_qkv1, grad_proj1)
-    smalls1 = small_sum(
-        jnp.concatenate([gain_attn1[None], gain_expert[None], grad_router.T], axis=0)
-    )
-    grad2, attn1_pair, grad_ex_up = lax.optimization_barrier((grad2, attn1_pair, grad_ex_up))
-    attn1_sum = far_sum(attn1_pair)
-    grad1, grad_up, grad_down, gain_dense = dense_backward(
-        grad2, norm_gains[0, 1], up_w, down_w, dense_state
-    )
-    down_pair = near_sum(row_parts(grad_down, 0))
-    up_pair = near_sum(row_parts(grad_up, 1))
-    grad1, down_pair, up_pair, attn1_sum, smalls1 = lax.optimization_barrier(
-        (grad1, down_pair, up_pair, attn1_sum, smalls1)
-    )
-    attn1_part = dp_halve(dp_rows(attn1_sum, smalls1), bits[0])
-    down_sum = far_sum(down_pair)
+    grad2_b = grad2.astype(bf16)
+    far_grad2 = far(grad2_b)
+    attn1_pair = own_pair((grad_qkv1, 1), (grad_proj1, 0))
+    far_grad2, attn1_pair = join(far_grad2, attn1_pair)
+    grad2_all = jnp.concatenate(near(grad2_b, far_grad2), axis=0)
+    unused_out, gelu_back = jax.vjp(jax.nn.gelu, dense_pre)
+    dense_grad = gelu_back(matmul_nt(grad2_all, dense_down))[0].astype(bf16)
+    dense_grad_pair = near_sum(row_parts(matmul_nt(dense_grad, dense_up).astype(bf16), 0))
+    branch_sum = far_sum(near_sum(row_parts(branch, 0)), far_grad2)
+    dense_grad_pair, branch_sum = join(dense_grad_pair, branch_sum)
+    grad_normed_m = far_sum(dense_grad_pair)
+    attn1_sum = far_sum(attn1_pair, grad_normed_m)
+    grad_up = matmul_tn(normed_m, dense_grad).astype(bf16)
+    grad_down = matmul_tn(dense_hidden, grad2_all).astype(bf16)
+    grad_normed_m, grad_up, grad_down = join(grad_normed_m, grad_up, grad_down)
+    dense_parts = halve_both((dp_rows(grad_up), dp_rows(grad_down)), 0)
+    grad_in, gain_dense = norm_backward(
+        grad_normed_m.astype(f32), norm_gains[0, 1], dense_unit, dense_inverse
+    )
+    grad1 = grad2 + grad_in
 
     def between(values):
-        nonlocal attn1_part, down_sum
-        values, attn1_part, down_sum = lax.optimization_barrier((values, attn1_part, down_sum))
+        nonlocal dense_parts
+        values, dense_parts = join(values, dense_parts)
+        dense_parts = halve_both(dense_parts, 1)
         return values
 
     grad0, grad_qkv0, grad_proj0, gain_attn0 = attention_backward(
         grad1, norm_gains[0, 0], qkv0, proj0, attn0_state, between
     )
-    attn1_part = dp_halves(attn1_part, bits[1:])
-    down_part = dp_halve(dp_rows(down_sum), bits[0])
-    attn0_pair = attn_pair(grad_qkv0, grad_proj0)
-    smalls0 = small_sum(jnp.concatenate([gain_attn0[None], gain_dense[None]], axis=0))
-    up_sum = far_sum(up_pair, down_sum)
-    attn0_sum = far_sum(attn0_pair, up_sum)
-    down_part = dp_halves(down_part, bits[1:])
-    up_part = dp_halves(dp_rows(up_sum), bits)
-    attn0_part = dp_halves(dp_rows(attn0_sum, smalls0), bits)
-    sums1 = dp_doubles(attn1_part, bits).astype(f32)
-    sums_down = dp_doubles(down_part, bits).astype(f32)
-    sums_up = dp_doubles(up_part, bits).astype(f32)
-    sums0 = dp_doubles(attn0_part, bits).astype(f32)
+    attn0_pair = own_pair((grad_qkv0, 1), (grad_proj0, 0))
+    smalls = small_sum(
+        jnp.concatenate(
+            [gain_attn0[None], gain_dense[None], gain_attn1[None], gain_expert[None], grad_router.T],
+            axis=0,
+        )
+    )
+    grad0, dense_parts, attn1_sum, attn0_pair, smalls = join(
+        grad0, dense_parts, attn1_sum, attn0_pair, smalls
+    )
+    attn0_sum = far_sum(attn0_pair)
+    attn_sums = lax.psum(jnp.concatenate([attn0_sum, attn1_sum, smalls], axis=0), "dp")
+    for step in range(2, last + 1):
+        dense_parts = halve_both(dense_parts, step)
+    for step in range(last, -1, -1):
+        dense_parts = double_both(dense_parts, step)
+    dense_up_sum = dense_parts[0][: dense_up.shape[0]].astype(f32)
+    dense_down_sum = dense_parts[1][: dense_down.shape[0]].astype(f32)
 
     grad0_b = grad0.astype(bf16)
     far_grad0 = far(grad0_b, attn0_sum)
+    stream4 = (stream3 + branch_sum.astype(f32)).astype(bf16)
+    far_stream4 = far(stream4, far_grad0)
+    grad_ex_up = far_sum(ex_up_pair, far_stream4)
     input_grad = in_order(near(grad0_b, far_grad0), me).astype(f32)
-    branch_sum = far_sum(near_sum(row_parts(branch, 0)), far_grad0)
-    stream4 = (stream3 + branch_sum.astype(f32)).astype(bf16)
-    block_output = in_order(near(stream4, far(stream4)), me)
+    block_output = in_order(near(stream4, far_stream4), me)
+    attn_sums, block_output, input_grad, grad_ex_up, dense_up_sum, dense_down_sum = join(
+        attn_sums, block_output, input_grad, grad_ex_up, dense_up_sum, dense_down_sum
+    )
+    attn_sums = attn_sums.astype(f32)
+    sums0, sums1 = attn_sums[: 4 * columns], attn_sums[4 * columns : 8 * columns]
 
     grad_qkv = jnp.stack(
         [
@@ -497,16 +534,17 @@
         ]
     )
     grad_proj = jnp.stack([sums[3 * columns : 4 * columns] for sums in (sums0, sums1)])
-    grad_gains = jnp.stack([sums[4 * columns : 4 * columns + 2] for sums in (sums0, sums1)])
-    router_grad = sums1[4 * columns + 2 : 4 * columns + 2 + experts].T
+    smalls = attn_sums[8 * columns :]
+    grad_gains = smalls[:4].reshape(2, 2, width)
+    router_grad = smalls[4 : 4 + experts].T
     return (
         block_output,
         input_grad,
         grad_gains,
         grad_qkv,
         grad_proj,
-        sums_up,
-        sums_down,
+        dense_up_sum,
+        dense_down_sum,
         router_grad,
         grad_ex_up.astype(f32)[None],
         grad_ex_down.astype(f32)[None],

time: 747 us -> 666 us (0.89)
  waiting for transfers between devices: 394 us -> 246 us
  other arithmetic: 48.7 us -> 89.8 us
  between operations: 4.12 us -> 16.8 us
  local copies, waits for them, and re-layouts: 47.7 us -> 58.4 us
  starting transfers between devices: 87.2 us -> 78.1 us
  matrix products: 131 us -> 140 us
    ppermute x24 -> x12, waiting for transfers between devices: 120 us -> 32.1 us  [dp_flip(): lax.ppermute(values, 'dp', [(i, i ^ 1 << bit) for i in range(groups)])]
    ppermute x68 -> x70, waiting for transfers between devices: 228 us -> 149 us  [flip(): return lax.ppermute(values, 'tensor', [(i, i ^ mask) for i in range(ranks)])]
    psum x0 -> x1, waiting for transfers between devices: none -> 63 us  [on_device(): lax.psum(jnp.concatenate([attn0_sum, attn1_sum, smalls], axis=0), 'dp')]
    all_to_all x4, waiting for transfers between devices: 45.5 us -> 2.32 us  [all_to_all(): lax.all_to_all(split_rows, 'dp', split_axis=0, concat_axis=0, tiled=True)]
    ppermute x24 -> x12, starting transfers between devices: 28.4 us -> 17.5 us  [dp_flip(): lax.ppermute(values, 'dp', [(i, i ^ 1 << bit) for i in range(groups)])]
    convert_element_type x32 -> x24, other arithmetic: 14.8 us -> 21.4 us  [add_rounded(): return (left_side.astype(f32) + right_side.astype(f32)).astype(bf16)]
    unnamed x179 -> x166, local copies, waits for them, and re-layouts: 16 us -> 12.9 us
    ppermute x68 -> x70, starting transfers between devices: 39.2 us -> 37.9 us  [flip(): return lax.ppermute(values, 'tensor', [(i, i ^ mask) for i in range(ranks)])]
  transfers between devices with their start and end apart: 96 -> 87, of which waited for: 43 -> 35; matrix products, arithmetic and copies ran while one was open for 22% -> 34% of each run, Pallas kernels for 2% -> 4%
where the time goes in v3:
time: 666 us; the launch traced here: 657 us
  waiting for transfers between devices  246 us (37%)
  matrix products  140 us (21%)
  other arithmetic  89.8 us (13%)
  starting transfers between devices  78.1 us (12%)
  local copies, waits for them, and re-layouts  58.4 us (9%)
  Pallas kernels  27.7 us (4%)
  between operations  16.8 us (3%)
    ppermute x70, waiting for transfers between devices, flip(): return lax.ppermute(values, 'tensor', [(i, i ^ mask) for i in range(ranks)])  149 us
    psum x1, waiting for transfers between devices, on_device(): lax.psum(jnp.concatenate([attn0_sum, attn1_sum, smalls], axis=0), 'dp')  63 us
    dot_general x8, matrix products, matmul(): return jnp.dot(left_side, right_side, preferred_element_type=f32)  40 us
    dot_general x6, matrix products, matmul_nt(): lax.dot_general(left_side, right_side, (((1,), (1,)), ((), ())), preferre...  39.8 us
    ppermute x70, starting transfers between devices, flip(): return lax.ppermute(values, 'tensor', [(i, i ^ mask) for i in range(ranks)])  37.9 us
    dot_general x8, matrix products, matmul_tn(): lax.dot_general(left_side, right_side, (((0,), (0,)), ((), ())), preferre...  36.2 us
    ppermute x12, waiting for transfers between devices, dp_flip(): lax.ppermute(values, 'dp', [(i, i ^ 1 << bit) for i in range(groups)])  32.1 us
    all_to_all x4, starting transfers between devices, all_to_all(): lax.all_to_all(split_rows, 'dp', split_axis=0, concat_axis=0, tiled=True)  22.6 us
  transfers between devices with their start and end apart: 87, of which 35 were waited for; matrix products, arithmetic and copies ran while one was open for 34% of the time, Pallas kernels for 4%

profile of v3, /device:TPU:0, one launch (start us, length us, event | category | flops | bytes accessed | tf_op | source)
XLA Modules:
  0.0 656.5 jit_solution(16791976643989254171)
XLA Ops:
  36.9 7.5 %collective-permute-done.4 = bf16[192,768]{1,0:T(8,128)(2,1)} collective-permute-done((bf16[192,768]{1,0:T(8,128)(2,1)}, bf16[192,768]{1,0:T(8,128)(2,1)}, u32[]{:S(2)}, u32[]{:S(2)}) %collective-permute-start.4) | collective-permute-done | bytes 294944 | tf_op jit(solution)/shard_map/ppermute | solution.py:36
  54.9 8.1 %collective-permute-done.6 = bf16[3,192,768]{2,1,0:T(8,128)(2,1)} collective-permute-done((bf16[3,192,768]{2,1,0:T(8,128)(2,1)}, bf16[3,192,768]{2,1,0:T(8,128)(2,1)}, u32[]{:S(2)}, u32[]{:S(2)}) %collective-permute-start.6) | collective-permute-done | bytes 884768 | tf_op jit(solution)/shard_map/ppermute | solution.py:36
  74.0 9.7 %collective-permute-done.8 = bf16[416,768]{1,0:T(8,128)(2,1)S(1)} collective-permute-done((bf16[416,768]{1,0:T(8,128)(2,1)S(1)}, bf16[416,768]{1,0:T(8,128)(2,1)S(1)}, u32[]{:S(2)}, u32[]{:S(2)}) %collective-permute-start.8) | collective-permute-done | bytes 639008 | tf_op jit(solution)/shard_map/ppermute | solution.py:36
  104.4 5.8 all-to-all-start
  120.5 6.4 collective-permute-done.16
  154.6 13.7 %collective-permute-done.19 = bf16[416,768]{1,0:T(8,128)(2,1)} collective-permute-done((bf16[416,768]{1,0:T(8,128)(2,1)}, bf16[416,768]{1,0:T(8,128)(2,1)}, u32[]{:S(2)}, u32[]{:S(2)}) %collective-permute-start.19) | collective-permute-done | bytes 639008 | tf_op jit(solution)/shard_map/ppermute | solution.py:36
  176.8 6.3 all-to-all-start.1
  188.0 25.1 %collective-permute-done.29 = bf16[768,768]{1,0:T(8,128)(2,1)} collective-permute-done((bf16[768,768]{1,0:T(8,128)(2,1)}, bf16[768,768]{1,0:T(8,128)(2,1)}, u32[]{:S(2)}, u32[]{:S(2)}) %collective-permute-start.29) | collective-permute-done | bytes 1179680 | tf_op jit(solution)/shard_map/ppermute | solution.py:36
  219.0 6.3 fusion.111
  225.4 12.9 %convolution_convert_fusion.11 = bf16[832,768]{1,0:T(8,128)(2,1)} fusion(bf16[768,768]{1,0:T(8,128)(2,1)} %collective-permute-done.30, bf16[768,768]{1,0:T(8,128)(2,1)} %collective-permute-done.29, bf16[768,768]{1,0:T(8,128)(2,1)} %collective-permute-done.28, bf16[768,768]{1,0:T(8,128)(2,1)} %bitcast.34, f32[832,3072]{1,0:T(8,128)S(1)} %fusion.111), kind=kOutput, calls=%fused_computation.97 | convolution fusion | flops 3968385024 | bytes 16220160 | tf_op jit(solution)/shard_map/dot_general | solution.py:19
  238.3 6.2 all-to-all-start.2
  244.6 10.1 %convolution_convert_fusion.1 = bf16[3072,768]{1,0:T(8,128)(2,1)S(1)} fusion(bf16[832,768]{1,0:T(8,128)(2,1)} %multiply_convert_fusion.2, f32[832,3072]{1,0:T(8,128)} %copy-done.75), kind=kOutput, calls=%fused_computation.29 | convolution fusion | flops 3951230976 | bytes 16220160 | tf_op jit(solution)/shard_map/dot_general | solution.py:23
  256.0 16.3 %fusion.6 = bf16[832,3072]{1,0:T(8,128)(2,1)} fusion(f32[832,3072]{1,0:T(8,128)} %copy-done.75, bf16[832,768]{1,0:T(8,128)(2,1)S(1)} %copy-done.31, bf16[768,768]{1,0:T(8,128)(2,1)} %collective-permute-done.30, bf16[768,768]{1,0:T(8,128)(2,1)} %collective-permute-done.29, bf16[768,768]{1,0:T(8,128)(2,1)} %collective-permute-done.28, ...), kind=kOutput, calls=%fused_computation.8 | convolution fusion | flops 3995860992 | bytes 21331968 | tf_op jit(solution)/shard_map/dot_general | solution.py:29
  280.4 9.1 %convolution_convert_fusion.10 = bf16[832,768]{1,0:T(8,128)(2,1)} fusion(bf16[832,3072]{1,0:T(8,128)(2,1)} %fusion.6, bf16[768,3072]{1,0:T(8,128)(2,1)} %pad_maximum_fusion), kind=kOutput, calls=%fused_computation.96 | convolution fusion | flops 3926507520 | bytes 11108352 | tf_op jit(solution)/shard_map/dot_general | solution.py:29
  293.9 6.5 convolution_convert_fusion.5
  301.2 7.3 %collective-permute-done.36 = bf16[768,768]{1,0:T(8,128)(2,1)} collective-permute-done((bf16[768,768]{1,0:T(8,128)(2,1)}, bf16[768,768]{1,0:T(8,128)(2,1)}, u32[]{:S(2)}, u32[]{:S(2)}) %collective-permute-start.36) | collective-permute-done | bytes 1179680 | tf_op jit(solution)/shard_map/ppermute | solution.py:36
  311.1 7.8 %convolution_convert_fusion = bf16[768,3072]{1,0:T(8,128)(2,1)S(1)} fusion(bf16[832,768]{1,0:T(8,128)(2,1)} %bitcast.30, bf16[832,3072]{1,0:T(8,128)(2,1)} %fusion.6), kind=kOutput, calls=%fused_computation.28 | convolution fusion | flops 3928227840 | bytes 11108352 | tf_op jit(solution)/shard_map/dot_general | solution.py:23
  325.8 4.9 convolution_convert_fusion.4
  345.7 9.0 %collective-permute-done.41 = bf16[416,768]{1,0:T(8,128)(2,1)} collective-permute-done((bf16[416,768]{1,0:T(8,128)(2,1)}, bf16[416,768]{1,0:T(8,128)(2,1)}, u32[]{:S(2)}, u32[]{:S(2)}) %collective-permute-start.41) | collective-permute-done | bytes 639008 | tf_op jit(solution)/shard_map/ppermute | solution.py:36
  360.5 10.2 %shard_map.197 = bf16[3,2,208,768]{3,2,1,0:T(8,128)(2,1)S(1)} custom-call(bf16[3,2,208,768]{3,2,1,0:T(8,128)(2,1)S(1)} %bitcast.179, bf16[416,768]{1,0:T(8,128)(2,1)S(1)} %convolution_convert_fusion.17.grad_ref), custom_call_target="tpu_custom_call" | custom-call | flops 664535040 | bytes 4472832 | tf_op jit(solution)/shard_map/pallas_call | solution.py:207
  383.0 12.8 %collective-permute-done.43 = bf16[416,768]{1,0:T(8,128)(2,1)S(1)} collective-permute-done((bf16[416,768]{1,0:T(8,128)(2,1)S(1)}, bf16[416,768]{1,0:T(8,128)(2,1)S(1)}, u32[]{:S(2)}, u32[]{:S(2)}) %collective-permute-start.43) | collective-permute-done | bytes 639008 | tf_op jit(solution)/shard_map/ppermute | solution.py:36
  399.4 8.4 %fusion.17 = bf16[1664,768]{1,0:T(8,128)(2,1)S(1)} fusion(f32[1664,768]{1,0:T(8,128)S(1)} %bitcast.214, bf16[768,768]{1,0:T(8,128)(2,1)S(1)} %copy-done.58, bf16[416,768]{1,0:T(8,128)(2,1)S(1)} %collective-permute-done.48, bf16[416,768]{1,0:T(8,128)(2,1)S(1)} %collective-permute-done.43, bf16[416,768]{1,0:T(8,128)(2,1)S(1)} %collective-permute-done.42, ...), kind=kOutput, calls=%fused_computation.26 | convolution fusion | flops 1998716928 | bytes 11403264 | tf_op jit(solution)/shard_map/dot_general | solution.py:29
  422.0 11.9 %collective-permute-done.54 = bf16[416,768]{1,0:T(8,128)(2,1)S(1)} collective-permute-done((bf16[416,768]{1,0:T(8,128)(2,1)S(1)}, bf16[416,768]{1,0:T(8,128)(2,1)S(1)}, u32[]{:S(2)}, u32[]{:S(2)}) %collective-permute-start.54) | collective-permute-done | bytes 639008 | tf_op jit(solution)/shard_map/ppermute | solution.py:36
  441.5 10.4 %shard_map.198 = bf16[3,2,208,768]{3,2,1,0:T(8,128)(2,1)S(1)} custom-call(bf16[3,2,208,768]{3,2,1,0:T(8,128)(2,1)S(1)} %bitcast.177, bf16[416,768]{1,0:T(8,128)(2,1)S(1)} %convolution_convert_fusion.16.grad_ref), custom_call_target="tpu_custom_call" | custom-call | flops 664535040 | bytes 4472832 | tf_op jit(solution)/shard_map/pallas_call | solution.py:207
  482.2 9.6 %collective-permute-done.74 = bf16[96,768]{1,0:T(8,128)(2,1)S(1)} collective-permute-done((bf16[96,768]{1,0:T(8,128)(2,1)S(1)}, bf16[96,768]{1,0:T(8,128)(2,1)S(1)}, u32[]{:S(2)}, u32[]{:S(2)}) %collective-permute-start.74) | collective-permute-done | bytes 147488 | tf_op jit(solution)/shard_map/ppermute | solution.py:74
  495.0 6.2 collective-permute-done.75
  505.8 5.3 collective-permute-done.76
  522.9 6.7 %collective-permute-done.68 = bf16[416,768]{1,0:T(8,128)(2,1)} collective-permute-done((bf16[416,768]{1,0:T(8,128)(2,1)}, bf16[416,768]{1,0:T(8,128)(2,1)}, u32[]{:S(2)}, u32[]{:S(2)}) %collective-permute-start.68) | collective-permute-done | bytes 639008 | tf_op jit(solution)/shard_map/ppermute | solution.py:36
  531.8 7.6 %collective-permute-done.81 = bf16[384,768]{1,0:T(8,128)(2,1)} collective-permute-done((bf16[384,768]{1,0:T(8,128)(2,1)}, bf16[384,768]{1,0:T(8,128)(2,1)}, u32[]{:S(2)}, u32[]{:S(2)}) %collective-permute-start.81) | collective-permute-done | bytes 589856 | tf_op jit(solution)/shard_map/ppermute | solution.py:74
  549.9 5.2 reshape.432
  562.9 7.2 %collective-permute-done.73 = bf16[768,768]{1,0:T(8,128)(2,1)} collective-permute-done((bf16[768,768]{1,0:T(8,128)(2,1)}, bf16[768,768]{1,0:T(8,128)(2,1)}, u32[]{:S(2)}, u32[]{:S(2)}) %collective-permute-start.73) | collective-permute-done | bytes 1179680 | tf_op jit(solution)/shard_map/ppermute | solution.py:36
  572.6 63.0 %all-reduce.12.cloned.1.call-done = bf16[1548,768]{1,0:T(8,128)(2,1)} async-done(((bf16[1548,768]{1,0:T(8,128)(2,1)}), bf16[1548,768]{1,0:T(8,128)(2,1)}) %all-reduce.12.cloned.1.call-update) | async-done | bytes 2377744 | tf_op jit(solution)/shard_map/psum | solution.py:509
  (542 shorter events, 296.2 us)
Async XLA Ops:
  10.1 22.9 %collective-permute-start.1 = (bf16[3,192,768]{2,1,0:T(8,128)(2,1)}, bf16[3,192,768]{2,1,0:T(8,128)(2,1)}, u32[]{:S(2)}, u32[]{:S(2)}) collective-permute-start(bf16[3,192,768]{2,1,0:T(8,128)(2,1)} %get-tuple-element.205), channel_id=1, source_target_pairs={{0,2},{1,3},{2,0},{3,1},{4,6},{5,7},{6,4},{7,5},{8,10},{9,11},{10,... | collective-permute-start | bytes 2654216 | tf_op jit(solution)/shard_map/ppermute | solution.py:36
  13.1 31.3 %collective-permute-start = (bf16[3,192,768]{2,1,0:T(8,128)(2,1)}, bf16[3,192,768]{2,1,0:T(8,128)(2,1)}, u32[]{:S(2)}, u32[]{:S(2)}) collective-permute-start(bf16[3,192,768]{2,1,0:T(8,128)(2,1)} %get-tuple-element.205), channel_id=1, source_target_pairs={{0,1},{1,0},{2,3},{3,2},{4,5},{5,4},{6,7},{7,6},{8,9},{9,8},{10,11... | collective-permute-start | bytes 2654216 | tf_op jit(solution)/shard_map/ppermute | solution.py:36
  14.0 37.8 %collective-permute-start.3 = (bf16[192,768]{1,0:T(8,128)(2,1)}, bf16[192,768]{1,0:T(8,128)(2,1)}, u32[]{:S(2)}, u32[]{:S(2)}) collective-permute-start(bf16[192,768]{1,0:T(8,128)(2,1)} %get-tuple-element.75), channel_id=1, source_target_pairs={{0,1},{1,0},{2,3},{3,2},{4,5},{5,4},{6,7},{7,6},{8,9},{9,8},{10,11... | collective-permute-start | bytes 884744 | tf_op jit(solution)/shard_map/ppermute | solution.py:36
  36.5 26.5 %collective-permute-start.6 = (bf16[3,192,768]{2,1,0:T(8,128)(2,1)}, bf16[3,192,768]{2,1,0:T(8,128)(2,1)}, u32[]{:S(2)}, u32[]{:S(2)}) collective-permute-start(bf16[3,192,768]{2,1,0:T(8,128)(2,1)} %get-tuple-element.77), channel_id=1, source_target_pairs={{0,2},{1,3},{2,0},{3,1},{4,6},{5,7},{6,4},{7,5},{8,10},{9,11},{10,... | collective-permute-start | bytes 2654216 | tf_op jit(solution)/shard_map/ppermute | solution.py:36
  95.5 33.1 %collective-permute-start.13 = (bf16[3,192,768]{2,1,0:T(8,128)(2,1)S(1)}, bf16[3,192,768]{2,1,0:T(8,128)(2,1)}, u32[]{:S(2)}, u32[]{:S(2)}) collective-permute-start(bf16[3,192,768]{2,1,0:T(8,128)(2,1)S(1)} %copy-done.37), channel_id=1, source_target_pairs={{0,1},{1,0},{2,3},{3,2},{4,5},{5,4},{6,7},{7,6},{8,9},{9,8},{10,11... | collective-permute-start | bytes 2654216 | tf_op jit(solution)/shard_map/ppermute | solution.py:36
  95.7 41.3 %collective-permute-start.15 = (bf16[192,768]{1,0:T(8,128)(2,1)}, bf16[192,768]{1,0:T(8,128)(2,1)}, u32[]{:S(2)}, u32[]{:S(2)}) collective-permute-start(bf16[192,768]{1,0:T(8,128)(2,1)} %get-tuple-element.81), channel_id=1, source_target_pairs={{0,1},{1,0},{2,3},{3,2},{4,5},{5,4},{6,7},{7,6},{8,9},{9,8},{10,11... | collective-permute-start | bytes 884744 | tf_op jit(solution)/shard_map/ppermute | solution.py:36
  104.4 36.6 %all-to-all-start = ((bf16[8,104,768]{2,1,0:T(8,128)(2,1)}), bf16[8,104,768]{2,1,0:T(8,128)(2,1)}, u32[]{:S(2)}, u32[]{:S(2)}) async-start(bf16[8,104,768]{2,1,0:T(8,128)(2,1)} %bitcast.188), calls=%async_computation | async-start | bytes 2555904 | tf_op jit(solution)/shard_map/all_to_all | solution.py:268
  152.8 17.5 %collective-permute-start.23 = (bf16[416,768]{1,0:T(8,128)(2,1)}, bf16[416,768]{1,0:T(8,128)(2,1)}, u32[]{:S(2)}, u32[]{:S(2)}) collective-permute-start(bf16[416,768]{1,0:T(8,128)(2,1)} %copy-done.17), channel_id=1, source_target_pairs={{0,1},{1,0},{2,3},{3,2},{4,5},{5,4},{6,7},{7,6},{8,9},{9,8},{10,11... | collective-permute-start | bytes 1916936 | tf_op jit(solution)/shard_map/ppermute | solution.py:36
  176.8 38.8 %all-to-all-start.1 = ((bf16[8,104,768]{2,1,0:T(8,128)(2,1)}), bf16[8,104,768]{2,1,0:T(8,128)(2,1)}, u32[]{:S(2)}, u32[]{:S(2)}) async-start(bf16[8,104,768]{2,1,0:T(8,128)(2,1)} %select_select_fusion), calls=%async_computation.1 | async-start | bytes 2555904 | tf_op jit(solution)/shard_map/all_to_all | solution.py:268
  183.1 30.0 %collective-permute-start.25 = (bf16[768,768]{1,0:T(8,128)(2,1)}, bf16[768,768]{1,0:T(8,128)(2,1)S(1)}, u32[]{:S(2)}, u32[]{:S(2)}) collective-permute-start(bf16[768,768]{1,0:T(8,128)(2,1)} %bitcast.189), channel_id=1, source_target_pairs={{0,1},{1,0},{2,3},{3,2},{4,5},{5,4},{6,7},{7,6},{8,9},{9,8},{10,11... | collective-permute-start | bytes 3538952 | tf_op jit(solution)/shard_map/ppermute | solution.py:36
  184.7 28.4 %collective-permute-start.29 = (bf16[768,768]{1,0:T(8,128)(2,1)}, bf16[768,768]{1,0:T(8,128)(2,1)}, u32[]{:S(2)}, u32[]{:S(2)}) collective-permute-start(bf16[768,768]{1,0:T(8,128)(2,1)} %bitcast.34), channel_id=1, source_target_pairs={{0,2},{1,3},{2,0},{3,1},{4,6},{5,7},{6,4},{7,5},{8,10},{9,11},{10,... | collective-permute-start | bytes 3538952 | tf_op jit(solution)/shard_map/ppermute | solution.py:36
  187.4 25.7 %collective-permute-start.27 = (bf16[768,768]{1,0:T(8,128)(2,1)S(1)}, bf16[768,768]{1,0:T(8,128)(2,1)S(1)}, u32[]{:S(2)}, u32[]{:S(2)}) collective-permute-start(bf16[768,768]{1,0:T(8,128)(2,1)S(1)} %constant_dynamic-update-slice_fusion), channel_id=1, source_target_pairs={{0,1},{1,0},{2,3},{3,2},{4,5},{5,4},{6,7},{7,6},{8,9},{9,8},{10,11... | collective-permute-start | bytes 3538952 | tf_op jit(solution)/shard_map/ppermute | solution.py:36
  187.5 37.9 %collective-permute-start.28 = (bf16[768,768]{1,0:T(8,128)(2,1)}, bf16[768,768]{1,0:T(8,128)(2,1)}, u32[]{:S(2)}, u32[]{:S(2)}) collective-permute-start(bf16[768,768]{1,0:T(8,128)(2,1)} %bitcast.34), channel_id=1, source_target_pairs={{0,1},{1,0},{2,3},{3,2},{4,5},{5,4},{6,7},{7,6},{8,9},{9,8},{10,11... | collective-permute-start | bytes 3538952 | tf_op jit(solution)/shard_map/ppermute | solution.py:36
  238.3 37.6 %all-to-all-start.2 = ((bf16[8,104,768]{2,1,0:T(8,128)(2,1)}), bf16[8,104,768]{2,1,0:T(8,128)(2,1)}, u32[]{:S(2)}, u32[]{:S(2)}) async-start(bf16[8,104,768]{2,1,0:T(8,128)(2,1)} %bitcast.197), calls=%async_computation.2 | async-start | bytes 2555904 | tf_op jit(solution)/shard_map/all_to_all | solution.py:268
  254.8 17.4 %collective-permute-start.32 = (bf16[768,768]{1,0:T(8,128)(2,1)S(1)}, bf16[768,768]{1,0:T(8,128)(2,1)S(1)}, u32[]{:S(2)}, u32[]{:S(2)}) collective-permute-start(bf16[768,768]{1,0:T(8,128)(2,1)S(1)} %get-tuple-element.174), channel_id=1, source_target_pairs={{0,1},{1,0},{2,3},{3,2},{4,5},{5,4},{6,7},{7,6},{8,9},{9,8},{10,11... | collective-permute-start | bytes 3538952 | tf_op jit(solution)/shard_map/ppermute | solution.py:36
  255.1 17.1 %collective-permute-start.31 = (bf16[768,768]{1,0:T(8,128)(2,1)S(1)}, bf16[768,768]{1,0:T(8,128)(2,1)S(1)}, u32[]{:S(2)}, u32[]{:S(2)}) collective-permute-start(bf16[768,768]{1,0:T(8,128)(2,1)S(1)} %get-tuple-element.175), channel_id=1, source_target_pairs={{0,1},{1,0},{2,3},{3,2},{4,5},{5,4},{6,7},{7,6},{8,9},{9,8},{10,11... | collective-permute-start | bytes 3538952 | tf_op jit(solution)/shard_map/ppermute | solution.py:36
  278.4 22.6 %collective-permute-start.34 = (f32[832]{0:T(1024)S(1)}, f32[832]{0:T(1024)S(1)}, u32[]{:S(2)}, u32[]{:S(2)}) collective-permute-start(f32[832]{0:T(1024)S(1)} %fusion.30), channel_id=1, source_target_pairs={{0,2},{1,3},{2,0},{3,1},{4,6},{5,7},{6,4},{7,5},{8,10},{9,11},{10,... | collective-permute-start | bytes 9992 | tf_op jit(solution)/shard_map/ppermute | solution.py:36
  279.8 40.4 %collective-permute-start.33 = (f32[832]{0:T(1024)S(1)}, f32[832]{0:T(1024)S(1)}, u32[]{:S(2)}, u32[]{:S(2)}) collective-permute-start(f32[832]{0:T(1024)S(1)} %fusion.30), channel_id=1, source_target_pairs={{0,1},{1,0},{2,3},{3,2},{4,5},{5,4},{6,7},{7,6},{8,9},{9,8},{10,11... | collective-permute-start | bytes 9992 | tf_op jit(solution)/shard_map/ppermute | solution.py:36
  279.8 28.7 %collective-permute-start.36 = (bf16[768,768]{1,0:T(8,128)(2,1)}, bf16[768,768]{1,0:T(8,128)(2,1)}, u32[]{:S(2)}, u32[]{:S(2)}) collective-permute-start(bf16[768,768]{1,0:T(8,128)(2,1)} %get-tuple-element.102), channel_id=1, source_target_pairs={{0,2},{1,3},{2,0},{3,1},{4,6},{5,7},{6,4},{7,5},{8,10},{9,11},{10,... | collective-permute-start | bytes 3538952 | tf_op jit(solution)/shard_map/ppermute | solution.py:36
  289.5 36.3 %all-to-all-start.3 = ((bf16[8,104,768]{2,1,0:T(8,128)(2,1)}), bf16[8,104,768]{2,1,0:T(8,128)(2,1)}, u32[]{:S(2)}, u32[]{:S(2)}) async-start(bf16[8,104,768]{2,1,0:T(8,128)(2,1)} %bitcast.196), calls=%async_computation.3 | async-start | bytes 2555904 | tf_op jit(solution)/shard_map/all_to_all | solution.py:268
  293.8 341.8 %all-reduce.12.cloned.1.call-start = ((), (), s32[]{:S(2)}) async-start(), calls=%async_computation.4 | async-start | bytes 4767744 | tf_op jit(solution)/shard_map/psum | solution.py:509
  301.0 19.8 %collective-permute-start.35 = (f32[832]{0:T(1024)S(1)}, f32[832]{0:T(1024)S(1)}, u32[]{:S(2)}, u32[]{:S(2)}) collective-permute-start(f32[832]{0:T(1024)S(1)} %collective-permute-done.34), channel_id=1, source_target_pairs={{0,1},{1,0},{2,3},{3,2},{4,5},{5,4},{6,7},{7,6},{8,9},{9,8},{10,11... | collective-permute-start | bytes 9992 | tf_op jit(solution)/shard_map/ppermute | solution.py:36
  344.3 54.0 %collective-permute-start.52 = (bf16[416,768]{1,0:T(8,128)(2,1)S(1)}, bf16[416,768]{1,0:T(8,128)(2,1)S(1)}, u32[]{:S(2)}, u32[]{:S(2)}) collective-permute-start(bf16[416,768]{1,0:T(8,128)(2,1)S(1)} %get-tuple-element.193), channel_id=1, source_target_pairs={{0,1},{1,0},{2,3},{3,2},{4,5},{5,4},{6,7},{7,6},{8,9},{9,8},{10,11... | collective-permute-start | bytes 1916936 | tf_op jit(solution)/shard_map/ppermute | solution.py:36
  380.1 19.2 %collective-permute-start.42 = (bf16[416,768]{1,0:T(8,128)(2,1)S(1)}, bf16[416,768]{1,0:T(8,128)(2,1)S(1)}, u32[]{:S(2)}, u32[]{:S(2)}) collective-permute-start(bf16[416,768]{1,0:T(8,128)(2,1)S(1)} %get-tuple-element.158), channel_id=1, source_target_pairs={{0,1},{1,0},{2,3},{3,2},{4,5},{5,4},{6,7},{7,6},{8,9},{9,8},{10,11... | collective-permute-start | bytes 1916936 | tf_op jit(solution)/shard_map/ppermute | solution.py:36
  434.9 17.9 %collective-permute-start.55 = (bf16[384,768]{1,0:T(8,128)(2,1)S(1)}, bf16[384,768]{1,0:T(8,128)(2,1)S(1)}, u32[]{:S(2)}, u32[]{:S(2)}) collective-permute-start(bf16[384,768]{1,0:T(8,128)(2,1)S(1)} %broadcast_select_fusion.5), channel_id=1, source_target_pairs={{0,4},{4,0},{8,12},{12,8},{16,20},{20,16},{24,28},{28,24},{1,5},{5... | collective-permute-start | bytes 1769480 | tf_op jit(solution)/shard_map/ppermute | solution.py:74
  436.9 38.2 %collective-permute-start.59 = (bf16[768,768]{1,0:T(8,128)(2,1)}, bf16[768,768]{1,0:T(8,128)(2,1)}, u32[]{:S(2)}, u32[]{:S(2)}) collective-permute-start(bf16[768,768]{1,0:T(8,128)(2,1)} %pad_maximum_fusion.13), channel_id=1, source_target_pairs={{0,2},{1,3},{2,0},{3,1},{4,6},{5,7},{6,4},{7,5},{8,10},{9,11},{10,... | collective-permute-start | bytes 3538952 | tf_op jit(solution)/shard_map/ppermute | solution.py:36
  477.8 35.7 %collective-permute-start.66 = (bf16[768,768]{1,0:T(8,128)(2,1)S(1)}, bf16[768,768]{1,0:T(8,128)(2,1)S(1)}, u32[]{:S(2)}, u32[]{:S(2)}) collective-permute-start(bf16[768,768]{1,0:T(8,128)(2,1)S(1)} %pad_maximum_fusion.15), channel_id=1, source_target_pairs={{0,2},{1,3},{2,0},{3,1},{4,6},{5,7},{6,4},{7,5},{8,10},{9,11},{10,... | collective-permute-start | bytes 3538952 | tf_op jit(solution)/shard_map/ppermute | solution.py:36
  512.0 18.4 %collective-permute-start.77 = (bf16[384,768]{1,0:T(8,128)(2,1)}, bf16[384,768]{1,0:T(8,128)(2,1)}, u32[]{:S(2)}, u32[]{:S(2)}) collective-permute-start(bf16[384,768]{1,0:T(8,128)(2,1)} %pad_maximum_fusion.23), channel_id=1, source_target_pairs={{0,4},{4,0},{8,12},{12,8},{16,20},{20,16},{24,28},{28,24},{1,5},{5... | collective-permute-start | bytes 1769480 | tf_op jit(solution)/shard_map/ppermute | solution.py:74
  515.6 23.7 %collective-permute-start.81 = (bf16[384,768]{1,0:T(8,128)(2,1)}, bf16[384,768]{1,0:T(8,128)(2,1)}, u32[]{:S(2)}, u32[]{:S(2)}) collective-permute-start(bf16[384,768]{1,0:T(8,128)(2,1)} %pad_maximum_fusion.24), channel_id=1, source_target_pairs={{0,8},{4,12},{8,0},{12,4},{16,24},{20,28},{24,16},{28,20},{1,9},{5... | collective-permute-start | bytes 1769480 | tf_op jit(solution)/shard_map/ppermute | solution.py:74
  520.7 34.4 %collective-permute-start.67 = (bf16[416,768]{1,0:T(8,128)(2,1)}, bf16[416,768]{1,0:T(8,128)(2,1)S(1)}, u32[]{:S(2)}, u32[]{:S(2)}) collective-permute-start(bf16[416,768]{1,0:T(8,128)(2,1)} %add_convert_fusion.12), channel_id=1, source_target_pairs={{0,1},{1,0},{2,3},{3,2},{4,5},{5,4},{6,7},{7,6},{8,9},{9,8},{10,11... | collective-permute-start | bytes 1916936 | tf_op jit(solution)/shard_map/ppermute | solution.py:36
  520.7 24.5 %collective-permute-start.71 = (bf16[416,768]{1,0:T(8,128)(2,1)}, bf16[416,768]{1,0:T(8,128)(2,1)}, u32[]{:S(2)}, u32[]{:S(2)}) collective-permute-start(bf16[416,768]{1,0:T(8,128)(2,1)} %multiply_add_fusion), channel_id=1, source_target_pairs={{0,1},{1,0},{2,3},{3,2},{4,5},{5,4},{6,7},{7,6},{8,9},{9,8},{10,11... | collective-permute-start | bytes 1916936 | tf_op jit(solution)/shard_map/ppermute | solution.py:36
  544.5 25.5 %collective-permute-start.73 = (bf16[768,768]{1,0:T(8,128)(2,1)}, bf16[768,768]{1,0:T(8,128)(2,1)}, u32[]{:S(2)}, u32[]{:S(2)}) collective-permute-start(bf16[768,768]{1,0:T(8,128)(2,1)} %get-tuple-element.130), channel_id=1, source_target_pairs={{0,2},{1,3},{2,0},{3,1},{4,6},{5,7},{6,4},{7,5},{8,10},{9,11},{10,... | collective-permute-start | bytes 3538952 | tf_op jit(solution)/shard_map/ppermute | solution.py:36
  (134 other events, 1181.0 us)
Sparse Core Ops, SparseCore 0:
  523.0 112.5 all-reduce.11
